TPU v7x, 256 devices: a whole 4x4x8 slice. The times are simulated.
256 devices in a mesh: ctx: 32 (over x, z), dec: 8 (over y, core).
Axes of the slice: x: 4, y: 4, z: 8, core: 2. Of those that a mesh axis runs over, the one named last changes fastest.
Arguments:
- queries: bfloat16 [512, 2, 8192], P(('ctx', 'dec')), may hold values from -256 to 256
- prompt_keys: bfloat16 [65536, 8, 128], P('ctx', 'dec'), may hold values from -40 to 40
- prompt_values: bfloat16 [65536, 8, 128], P('ctx', 'dec'), may hold values from -6 to 6
- suffix_keys: bfloat16 [512, 1024, 8, 128], P(('ctx', 'dec')), may hold values from -22 to 22
- suffix_values: bfloat16 [512, 1024, 8, 128], P(('ctx', 'dec')), may hold values from -6 to 6
- new_keys: bfloat16 [512, 2, 8, 128], P(('ctx', 'dec')), may hold values from -36 to 36
- new_values: bfloat16 [512, 2, 8, 128], P(('ctx', 'dec')), may hold values from -6 to 6
- lengths: int32 [512], P(('ctx', 'dec')), may hold values from 1 to 1024, as said below
Outputs:
- attended: bfloat16 [512, 2, 8192], P(('ctx', 'dec'))
Inputs may be any that keep to these rules, and one draw needn't show every extreme that they name: `lengths`: at least one sample has exactly 1024 cached suffix tokens in every draw.
All inputs are finite; a program needn't handle non-finite values.
Results may differ from a plain program's by a relative error of at most 0.003.
Values may be sent and summed in bfloat16 or wider, within the bound.
No kernel may reach another device: no remote copies, remote signals or barrier semaphores. Data moves between devices by JAX's collectives and lax.ppermute only.
A program may use at most 128 MiB of HBM per device.

v0:
```python
import jax
import jax.numpy as jnp
from jax import lax
from jax.sharding import PartitionSpec as P

MASKED_SCORE = -1e30


def block_part(scores, visible, values, form):
    masked = jnp.where(visible, scores, MASKED_SCORE)
    block_max = jnp.max(masked, axis=-1)
    weights = jnp.where(visible, jnp.exp(masked - block_max[..., None]), 0.0).astype(jnp.bfloat16)
    block_total = jnp.sum(weights, axis=-1, dtype=jnp.float32)
    block_sum = jnp.einsum(form, weights, values, preferred_element_type=jnp.float32)
    return (block_max, block_total, block_sum)


def merge_parts(left, right):
    highest = jnp.maximum(left[0], right[0])
    left_factor = jnp.exp(left[0] - highest)
    right_factor = jnp.exp(right[0] - highest)
    return (
        highest,
        left[1] * left_factor + right[1] * right_factor,
        left[2] * left_factor[..., None] + right[2] * right_factor[..., None],
    )


def combine_leading(moved):
    highest = jnp.max(moved[0], axis=0)
    factors = jnp.exp(moved[0] - highest[None])
    return (
        highest,
        jnp.sum(moved[1] * factors, axis=0),
        jnp.sum(moved[2] * factors[..., None], axis=0),
    )


def empty_state(state_shape, head_dim):
    return (
        jnp.full(state_shape, MASKED_SCORE, jnp.float32),
        jnp.zeros(state_shape, jnp.float32),
        jnp.zeros(state_shape + (head_dim,), jnp.float32),
    )


def prompt_part(rows, prompt_keys, prompt_values):
    row_count, step_count, groups, packed = rows.shape
    positions_here, _, head_dim = prompt_keys.shape
    grouped = rows.reshape(row_count, step_count, groups, packed // head_dim, head_dim)
    key_span = min(512, positions_here)
    key_blocks = prompt_keys.reshape(positions_here // key_span, key_span, groups, head_dim)
    value_blocks = prompt_values.reshape(positions_here // key_span, key_span, groups, head_dim)
    inverse_root = head_dim ** (-0.5)

    def prompt_step(carried, blocks_pair):
        scores = (
            jnp.einsum(
                "rtgqd,kgd->rtgqk", grouped, blocks_pair[0], preferred_element_type=jnp.float32
            )
            * inverse_root
        )
        return (
            merge_parts(carried, block_part(scores, True, blocks_pair[1], "rtgqk,kgd->rtgqd")),
            None,
        )

    initial = empty_state((row_count, step_count, groups, packed // head_dim), head_dim)
    result, _ = lax.scan(prompt_step, initial, (key_blocks, value_blocks))
    return result


def local(
    queries, prompt_keys, prompt_values, suffix_keys, suffix_values, new_keys, new_values, lengths
):
    own_rows, step_count, feature_width = queries.shape
    suffix_length, kv_heads, head_dim = (
        suffix_keys.shape[1],
        suffix_keys.shape[2],
        suffix_keys.shape[3],
    )
    per_group = feature_width // (kv_heads * head_dim)
    by_group = queries.reshape(own_rows, step_count, kv_heads, per_group * head_dim)
    local_rows = lax.all_to_all(by_group, "dec", split_axis=2, concat_axis=0, tiled=True)
    found = prompt_part(
        lax.all_gather(local_rows, "ctx", axis=0, tiled=True), prompt_keys, prompt_values
    )
    grouped = queries.reshape(own_rows, step_count, kv_heads, per_group, head_dim)
    inverse_root = head_dim ** (-0.5)
    suffix_span = min(512, suffix_length)

    def suffix_step(number, carried):
        offset = number * suffix_span
        keys_here = lax.dynamic_slice_in_dim(suffix_keys, offset, suffix_span, 1)
        values_here = lax.dynamic_slice_in_dim(suffix_values, offset, suffix_span, 1)
        scores = (
            jnp.einsum("stgqd,skgd->stgqk", grouped, keys_here, preferred_element_type=jnp.float32)
            * inverse_root
        )
        positions = offset + jnp.arange(suffix_span, dtype=jnp.int32)
        visible = (positions[None, :] < lengths[:, None])[:, None, None, None, :]
        return merge_parts(carried, block_part(scores, visible, values_here, "stgqk,skgd->stgqd"))

    own_initial = empty_state((own_rows, step_count, kv_heads, per_group), head_dim)
    suffix_state = lax.fori_loop(0, suffix_length // suffix_span, suffix_step, own_initial)
    scores = (
        jnp.einsum("stgqd,sugd->stgqu", grouped, new_keys, preferred_element_type=jnp.float32)
        * inverse_root
    )
    step_index = jnp.arange(step_count, dtype=jnp.int32)
    visible = (step_index[None, :] <= step_index[:, None])[None, :, None, None, :]
    suffix_state = merge_parts(
        suffix_state, block_part(scores, visible, new_values, "stgqu,sugd->stgqd")
    )
    moved = (
        lax.all_to_all(found[0][None], "ctx", split_axis=1, concat_axis=0, tiled=True),
        lax.all_to_all(found[1][None], "ctx", split_axis=1, concat_axis=0, tiled=True),
        lax.all_to_all(found[2][None], "ctx", split_axis=1, concat_axis=0, tiled=True),
    )
    mine = combine_leading(moved)
    prompt_mine = (
        lax.all_to_all(mine[0], "dec", split_axis=0, concat_axis=2, tiled=True),
        lax.all_to_all(mine[1], "dec", split_axis=0, concat_axis=2, tiled=True),
        lax.all_to_all(mine[2], "dec", split_axis=0, concat_axis=2, tiled=True),
    )
    combined = merge_parts(prompt_mine, suffix_state)
    attended = combined[2] / combined[1][..., None]
    return attended.astype(jnp.bfloat16).reshape(own_rows, step_count, feature_width)


def solution(mesh):
    return jax.shard_map(
        local,
        mesh=mesh,
        in_specs=(
            P(("ctx", "dec"), None, None),
            P("ctx", "dec", None),
            P("ctx", "dec", None),
            P(("ctx", "dec"), None, None, None),
            P(("ctx", "dec"), None, None, None),
            P(("ctx", "dec"), None, None, None),
            P(("ctx", "dec"), None, None, None),
            P(("ctx", "dec")),
        ),
        out_specs=P(("ctx", "dec"), None, None),
        check_vma=False,
    )
```

profile of v0, /device:TPU:1, one launch (start us, length us, event | category | flops | bytes accessed | tf_op | source)
XLA Modules:
  0.0 397.5 jit_solution(7699972492646926972)
XLA Ops:
  6.5 0.9 copy.125
  7.4 11.1 %all_to_all.111 = bf16[2,2,8,1024]{3,1,0,2:T(2,128)(2,1)} all-to-all(bf16[2,2,8,1024]{3,1,0,2:T(2,128)(2,1)S(1)} %bitcast.218), channel_id=1, replica_groups=mesh['ctx'=32,'dec'=8] {'dec'}, dimensions={2} | all-to-all | bytes 131072 | tf_op jit(solution)/shard_map/all_to_all | solution.py:84
  18.6 74.7 %all-gather.2.cloned.1.call-done = bf16[512,2,1,1024]{3,1,2,0:T(2,128)(2,1)} async-done(((bf16[16,2,1,1024]{3,1,2,0:T(2,128)(2,1)}), bf16[512,2,1,1024]{3,1,2,0:T(2,128)(2,1)}) %all-gather.2.cloned.1.call-update) | async-done | bytes 2097168 | tf_op jit(solution)/shard_map/all_gather | solution.py:86
  93.4 6.1 %copy.43 = bf16[512,2,1,1024]{0,3,1,2:T(8,128)(2,1)} copy(bf16[512,2,1,1024]{3,1,2,0:T(2,128)(2,1)} %all-gather.2.cloned.1.call-done) | data formatting | bytes 4194304 | tf_op jit(solution)/shard_map/all_gather | solution.py:86
  99.5 3.0 copy.44
  102.6 121.0 %while.33 = (s32[]{:T(128)}, f32[512,2,1,8]{0,3,1,2:T(8,128)S(1)}, f32[512,2,1,8]{0,3,1,2:T(8,128)S(1)}, f32[512,2,1,8,128]{0,4,3,1,2:T(8,128)}, bf16[4,512,1,12...) while((s32[]{:T(128)}, f32[512,2,1,8]{0,3,1,2:T(8,128)S(1)}, ...), condition=%wide.region_3.4_spmd.clone, body=%wide.region_0.3_spmd.clone.sunk | while | flops 2193686528 | bytes 61703268 | solution.py:69
  102.6 9.0 %bitcast_reduce_fusion.2 = (f32[512,2,8]{0,2,1:T(8,128)S(1)}, f32[512,512,2,8]{1,0,3,2:T(8,128)}) fusion(bf16[512,2,1,8,128]{4,0,3,1,2:T(8,128)(2,1)S(1)} %get-tuple-element.476, bf16[4,512,1,128]{3,1,2,0:T(8,128)(2,1)} %get-tuple-element.475, s32[]{:T(128)} %get-tuple-element.462), kind=kOutput, calls=%fused_computation.1.clone.1 | convolution fusion | flops 1082122240 | bytes 19038720 | tf_op jit(solution)/shard_map/while/body/eval_jaxpr/rtgqd,kgd->rtgqk/dot_general | solution.py:58
  111.6 8.8 %convert_reduce_fusion.5 = f32[512,2,8]{0,2,1:T(8,128)S(1)} fusion(f32[512,2,8]{0,2,1:T(8,128)S(1)} %get-tuple-element.431, f32[512,512,2,8]{1,0,3,2:T(8,128)} %get-tuple-element.433), kind=kLoop, calls=%fused_computation.4.clone.1 | loop fusion | flops 20963328 | bytes 16842752 | tf_op jit(solution)/shard_map/while/body/eval_jaxpr/reduce_sum | solution.py:13
  120.4 11.5 %bitcast_add_fusion.2 = f32[512,2,1,8,128]{0,4,3,1,2:T(8,128)} fusion(f32[512,2,1,8,128]{0,4,3,1,2:T(8,128)} %get-tuple-element.465, f32[512,2,8]{0,2,1:T(8,128)S(1)} %get-tuple-element.435, f32[512,2,8]{0,2,1:T(8,128)S(1)} %get-tuple-element.436, pred[]{:T(512)S(6)} %compare.6, f32[512,512,2,8]{1,0,3,2:T(8,128)} %get-tuple-element.433, ...), kind=kOutput, calls=%fused_computation.7.clone.1 | convolution fusion | flops 1090519040 | bytes 25395712 | tf_op jit(solution)/shard_map/while/body/eval_jaxpr/rtgqk,kgd->rtgqd/dot_general | solution.py:14
  131.9 9.0 %bitcast_reduce_fusion.2 = (f32[512,2,8]{0,2,1:T(8,128)S(1)}, f32[512,512,2,8]{1,0,3,2:T(8,128)}) fusion(bf16[512,2,1,8,128]{4,0,3,1,2:T(8,128)(2,1)S(1)} %get-tuple-element.476, bf16[4,512,1,128]{3,1,2,0:T(8,128)(2,1)} %get-tuple-element.475, s32[]{:T(128)} %get-tuple-element.462), kind=kOutput, calls=%fused_computation.1.clone.1 | convolution fusion | flops 1082122240 | bytes 19038720 | tf_op jit(solution)/shard_map/while/body/eval_jaxpr/rtgqd,kgd->rtgqk/dot_general | solution.py:58
  140.9 8.8 %convert_reduce_fusion.5 = f32[512,2,8]{0,2,1:T(8,128)S(1)} fusion(f32[512,2,8]{0,2,1:T(8,128)S(1)} %get-tuple-element.431, f32[512,512,2,8]{1,0,3,2:T(8,128)} %get-tuple-element.433), kind=kLoop, calls=%fused_computation.4.clone.1 | loop fusion | flops 20963328 | bytes 16842752 | tf_op jit(solution)/shard_map/while/body/eval_jaxpr/reduce_sum | solution.py:13
  149.7 12.7 %bitcast_add_fusion.2 = f32[512,2,1,8,128]{0,4,3,1,2:T(8,128)} fusion(f32[512,2,1,8,128]{0,4,3,1,2:T(8,128)} %get-tuple-element.465, f32[512,2,8]{0,2,1:T(8,128)S(1)} %get-tuple-element.435, f32[512,2,8]{0,2,1:T(8,128)S(1)} %get-tuple-element.436, pred[]{:T(512)S(6)} %compare.6, f32[512,512,2,8]{1,0,3,2:T(8,128)} %get-tuple-element.433, ...), kind=kOutput, calls=%fused_computation.7.clone.1 | convolution fusion | flops 1090519040 | bytes 25395712 | tf_op jit(solution)/shard_map/while/body/eval_jaxpr/rtgqk,kgd->rtgqd/dot_general | solution.py:14
  162.5 9.0 %bitcast_reduce_fusion.2 = (f32[512,2,8]{0,2,1:T(8,128)S(1)}, f32[512,512,2,8]{1,0,3,2:T(8,128)}) fusion(bf16[512,2,1,8,128]{4,0,3,1,2:T(8,128)(2,1)S(1)} %get-tuple-element.476, bf16[4,512,1,128]{3,1,2,0:T(8,128)(2,1)} %get-tuple-element.475, s32[]{:T(128)} %get-tuple-element.462), kind=kOutput, calls=%fused_computation.1.clone.1 | convolution fusion | flops 1082122240 | bytes 19038720 | tf_op jit(solution)/shard_map/while/body/eval_jaxpr/rtgqd,kgd->rtgqk/dot_general | solution.py:58
  171.5 8.8 %convert_reduce_fusion.5 = f32[512,2,8]{0,2,1:T(8,128)S(1)} fusion(f32[512,2,8]{0,2,1:T(8,128)S(1)} %get-tuple-element.431, f32[512,512,2,8]{1,0,3,2:T(8,128)} %get-tuple-element.433), kind=kLoop, calls=%fused_computation.4.clone.1 | loop fusion | flops 20963328 | bytes 16842752 | tf_op jit(solution)/shard_map/while/body/eval_jaxpr/reduce_sum | solution.py:13
  180.3 12.7 %bitcast_add_fusion.2 = f32[512,2,1,8,128]{0,4,3,1,2:T(8,128)} fusion(f32[512,2,1,8,128]{0,4,3,1,2:T(8,128)} %get-tuple-element.465, f32[512,2,8]{0,2,1:T(8,128)S(1)} %get-tuple-element.435, f32[512,2,8]{0,2,1:T(8,128)S(1)} %get-tuple-element.436, pred[]{:T(512)S(6)} %compare.6, f32[512,512,2,8]{1,0,3,2:T(8,128)} %get-tuple-element.433, ...), kind=kOutput, calls=%fused_computation.7.clone.1 | convolution fusion | flops 1090519040 | bytes 25395712 | tf_op jit(solution)/shard_map/while/body/eval_jaxpr/rtgqk,kgd->rtgqd/dot_general | solution.py:14
  193.0 9.0 %bitcast_reduce_fusion.2 = (f32[512,2,8]{0,2,1:T(8,128)S(1)}, f32[512,512,2,8]{1,0,3,2:T(8,128)}) fusion(bf16[512,2,1,8,128]{4,0,3,1,2:T(8,128)(2,1)S(1)} %get-tuple-element.476, bf16[4,512,1,128]{3,1,2,0:T(8,128)(2,1)} %get-tuple-element.475, s32[]{:T(128)} %get-tuple-element.462), kind=kOutput, calls=%fused_computation.1.clone.1 | convolution fusion | flops 1082122240 | bytes 19038720 | tf_op jit(solution)/shard_map/while/body/eval_jaxpr/rtgqd,kgd->rtgqk/dot_general | solution.py:58
  202.0 8.8 %convert_reduce_fusion.5 = f32[512,2,8]{0,2,1:T(8,128)S(1)} fusion(f32[512,2,8]{0,2,1:T(8,128)S(1)} %get-tuple-element.431, f32[512,512,2,8]{1,0,3,2:T(8,128)} %get-tuple-element.433), kind=kLoop, calls=%fused_computation.4.clone.1 | loop fusion | flops 20963328 | bytes 16842752 | tf_op jit(solution)/shard_map/while/body/eval_jaxpr/reduce_sum | solution.py:13
  210.8 12.7 %bitcast_add_fusion.2 = f32[512,2,1,8,128]{0,4,3,1,2:T(8,128)} fusion(f32[512,2,1,8,128]{0,4,3,1,2:T(8,128)} %get-tuple-element.465, f32[512,2,8]{0,2,1:T(8,128)S(1)} %get-tuple-element.435, f32[512,2,8]{0,2,1:T(8,128)S(1)} %get-tuple-element.436, pred[]{:T(512)S(6)} %compare.6, f32[512,512,2,8]{1,0,3,2:T(8,128)} %get-tuple-element.433, ...), kind=kOutput, calls=%fused_computation.7.clone.1 | convolution fusion | flops 1090519040 | bytes 25395712 | tf_op jit(solution)/shard_map/while/body/eval_jaxpr/rtgqk,kgd->rtgqd/dot_general | solution.py:14
  223.8 1.4 reshape.185
  225.3 5.0 %all-to-all-start.2 = ((f32[32,1,256]{2,1,0:T(1,128)}), f32[32,1,256]{2,1,0:T(1,128)S(1)}, u32[]{:S(2)}, u32[]{:S(2)}) async-start(f32[32,1,256]{2,1,0:T(1,128)} %reshape.185), calls=%async_computation.2 | async-start | bytes 65536 | tf_op jit(solution)/shard_map/all_to_all | solution.py:116
  230.6 1.4 reshape.187
  232.0 7.1 %all-to-all-done.2 = f32[32,1,256]{2,1,0:T(1,128)S(1)} async-done(((f32[32,1,256]{2,1,0:T(1,128)}), f32[32,1,256]{2,1,0:T(1,128)S(1)}, u32[]{:S(2)}, u32[]{:S(2)}) %all-to-all-start.2) | async-done | bytes 32800 | tf_op jit(solution)/shard_map/all_to_all | solution.py:116
  239.1 4.0 %all-to-all-start.5 = ((f32[32,1,256]{2,1,0:T(1,128)}), f32[32,1,256]{2,1,0:T(1,128)S(1)}, u32[]{:S(2)}, u32[]{:S(2)}) async-start(f32[32,1,256]{2,1,0:T(1,128)} %reshape.187), calls=%async_computation.5 | async-start | bytes 65536 | tf_op jit(solution)/shard_map/all_to_all | solution.py:117
  243.1 0.5 broadcast.165
  243.6 0.7 reduce.5
  244.4 0.8 reshape.186
  245.7 5.9 %all-to-all-done.5 = f32[32,1,256]{2,1,0:T(1,128)S(1)} async-done(((f32[32,1,256]{2,1,0:T(1,128)}), f32[32,1,256]{2,1,0:T(1,128)S(1)}, u32[]{:S(2)}, u32[]{:S(2)}) %all-to-all-start.5) | async-done | bytes 32800 | tf_op jit(solution)/shard_map/all_to_all | solution.py:117
  251.6 0.7 reduce.6
  252.4 0.8 reshape.188
  253.5 0.7 copy.63
  254.2 11.9 %all-to-all-start.6 = ((f32[16,2,1,8]{3,1,2,0:T(2,128)}), f32[16,2,1,8]{3,1,2,0:T(2,128)S(1)}, u32[]{:S(2)}, u32[]{:S(2)}) async-start(f32[16,2,1,8]{3,1,2,0:T(2,128)} %copy.63), calls=%async_computation.6 | async-start | bytes 32768 | tf_op jit(solution)/shard_map/all_to_all | solution.py:123
  266.1 5.4 %copy.46 = f32[512,2,1,8,128]{4,3,1,0,2:T(8,128)} copy(f32[512,2,1,8,128]{0,4,3,1,2:T(8,128)} %get-tuple-element.185) | data formatting | bytes 8388608 | tf_op jit(solution)/shard_map/while | solution.py:69
  271.5 5.0 %all-to-all-start.1 = ((f32[1,512,2,1,8,128]{5,4,2,3,0,1:T(8,128)}), f32[1,512,2,1,8,128]{5,4,2,3,0,1:T(8,128)}, u32[]{:S(2)}, u32[]{:S(2)}) async-start(f32[1,512,2,1,8,128]{5,4,2,3,0,1:T(8,128)} %bitcast.208), calls=%async_computation.1 | async-start | bytes 8388608 | tf_op jit(solution)/shard_map/all_to_all | solution.py:118
  277.2 8.5 %while.34 = (s32[]{:T(128)}, f32[2,2,8,8]{3,1,2,0:T(2,128)S(1)}, f32[2,2,8,8]{3,1,2,0:T(2,128)S(1)}, f32[2,2,8,8,128]{4,3,1,2,0:T(8,128)S(1)}, s32[2]{0:T(128)S(...) while((s32[]{:T(128)}, f32[2,2,8,8]{3,1,2,0:T(2,128)S(1)}, ...), condition=%wide.region_9.10_spmd.clone, body=%wide.region_6.0_spmd.clone.sunk | while | flops 68684800 | bytes 14506174 | solution.py:105
  277.3 2.5 constant_dynamic-slice_fusion.3
  279.9 0.8 fusion.65
  280.9 0.6 fusion.67
  281.5 2.5 constant_dynamic-slice_fusion.3
  284.1 0.8 fusion.65
  285.2 0.6 fusion.67
  286.0 0.7 copy.51
  287.1 84.4 %all-to-all-done.1 = f32[1,512,2,1,8,128]{5,4,2,3,0,1:T(8,128)} async-done(((f32[1,512,2,1,8,128]{5,4,2,3,0,1:T(8,128)}), f32[1,512,2,1,8,128]{5,4,2,3,0,1:T(8,128)}, u32[]{:S(2)}, u32[]{:S(2)}) %all-to-all-start.1) | async-done | bytes 4194336 | tf_op jit(solution)/shard_map/all_to_all | solution.py:118
  371.4 4.3 %all-to-all-start.4 = ((f32[16,2,1,8]{3,1,2,0:T(2,128)}), f32[16,2,1,8]{3,1,2,0:T(2,128)S(1)}, u32[]{:S(2)}, u32[]{:S(2)}) async-start(f32[16,2,1,8]{3,1,2,0:T(2,128)} %copy.51), calls=%async_computation.4 | async-start | bytes 32768 | tf_op jit(solution)/shard_map/all_to_all | solution.py:122
  375.7 3.5 multiply_reduce_fusion
  379.2 1.2 all-to-all-done.4
  380.4 4.0 %all-to-all-start.3 = ((f32[16,2,1,8,128]{4,3,1,2,0:T(8,128)}), f32[16,2,1,8,128]{4,3,1,2,0:T(8,128)S(1)}, u32[]{:S(2)}, u32[]{:S(2)}) async-start(f32[16,2,1,8,128]{4,3,1,2,0:T(8,128)} %bitcast.11), calls=%async_computation.3 | async-start | bytes 262144 | tf_op jit(solution)/shard_map/all_to_all | solution.py:124
  384.4 5.2 %all-to-all-done.3 = f32[16,2,1,8,128]{4,3,1,2,0:T(8,128)S(1)} async-done(((f32[16,2,1,8,128]{4,3,1,2,0:T(8,128)}), f32[16,2,1,8,128]{4,3,1,2,0:T(8,128)S(1)}, u32[]{:S(2)}, u32[]{:S(2)}) %all-to-all-start.3) | async-done | bytes 131104 | tf_op jit(solution)/shard_map/all_to_all | solution.py:124
  390.0 0.6 reshape.174
  (57 shorter events, 4.0 us)
Async XLA Ops:
  6.5 383.1 %copy-start = (bf16[2,2,8,128]{3,2,1,0:T(8,128)(2,1)S(1)}, bf16[2,2,8,128]{3,2,1,0:T(8,128)(2,1)}, u32[]{:S(2)}) copy-start(bf16[2,2,8,128]{3,2,1,0:T(8,128)(2,1)} %param.18) | copy-start | bytes 24580
  6.5 86.8 %all-gather.2.cloned.1.call-start = ((), (), s32[]{:S(2)}) async-start(), calls=%async_computation.7 | async-start | bytes 2162688 | tf_op jit(solution)/shard_map/all_gather | solution.py:86
  225.3 13.8 %all-to-all-start.2 = ((f32[32,1,256]{2,1,0:T(1,128)}), f32[32,1,256]{2,1,0:T(1,128)S(1)}, u32[]{:S(2)}, u32[]{:S(2)}) async-start(f32[32,1,256]{2,1,0:T(1,128)} %reshape.185), calls=%async_computation.2 | async-start | bytes 65536 | tf_op jit(solution)/shard_map/all_to_all | solution.py:116
  239.1 12.6 %all-to-all-start.5 = ((f32[32,1,256]{2,1,0:T(1,128)}), f32[32,1,256]{2,1,0:T(1,128)S(1)}, u32[]{:S(2)}, u32[]{:S(2)}) async-start(f32[32,1,256]{2,1,0:T(1,128)} %reshape.187), calls=%async_computation.5 | async-start | bytes 65536 | tf_op jit(solution)/shard_map/all_to_all | solution.py:117
  254.2 17.3 %all-to-all-start.6 = ((f32[16,2,1,8]{3,1,2,0:T(2,128)}), f32[16,2,1,8]{3,1,2,0:T(2,128)S(1)}, u32[]{:S(2)}, u32[]{:S(2)}) async-start(f32[16,2,1,8]{3,1,2,0:T(2,128)} %copy.63), calls=%async_computation.6 | async-start | bytes 32768 | tf_op jit(solution)/shard_map/all_to_all | solution.py:123
  271.5 5.0 %copy-start.1 = (bf16[2,2,8192]{2,1,0:T(2,128)(2,1)S(1)}, bf16[2,2,8192]{2,1,0:T(2,128)(2,1)}, u32[]{:S(2)}) copy-start(bf16[2,2,8192]{2,1,0:T(2,128)(2,1)} %param.12) | copy-start | bytes 196612
  271.5 5.2 %copy-start.3 = (bf16[2,2,8,128]{3,2,1,0:T(8,128)(2,1)S(1)}, bf16[2,2,8,128]{3,2,1,0:T(8,128)(2,1)}, u32[]{:S(2)}) copy-start(bf16[2,2,8,128]{3,2,1,0:T(8,128)(2,1)} %param.17) | copy-start | bytes 24580
  271.5 5.7 %copy-start.2 = (s32[2]{0:T(128)S(1)}, s32[2]{0:T(128)}, u32[]{:S(2)}) copy-start(s32[2]{0:T(128)} %param.19) | copy-start | bytes 28
  271.5 99.9 %all-to-all-start.1 = ((f32[1,512,2,1,8,128]{5,4,2,3,0,1:T(8,128)}), f32[1,512,2,1,8,128]{5,4,2,3,0,1:T(8,128)}, u32[]{:S(2)}, u32[]{:S(2)}) async-start(f32[1,512,2,1,8,128]{5,4,2,3,0,1:T(8,128)} %bitcast.208), calls=%async_computation.1 | async-start | bytes 8388608 | tf_op jit(solution)/shard_map/all_to_all | solution.py:118
  371.4 8.9 %all-to-all-start.4 = ((f32[16,2,1,8]{3,1,2,0:T(2,128)}), f32[16,2,1,8]{3,1,2,0:T(2,128)S(1)}, u32[]{:S(2)}, u32[]{:S(2)}) async-start(f32[16,2,1,8]{3,1,2,0:T(2,128)} %copy.51), calls=%async_computation.4 | async-start | bytes 32768 | tf_op jit(solution)/shard_map/all_to_all | solution.py:122
  380.4 9.3 %all-to-all-start.3 = ((f32[16,2,1,8,128]{4,3,1,2,0:T(8,128)}), f32[16,2,1,8,128]{4,3,1,2,0:T(8,128)S(1)}, u32[]{:S(2)}, u32[]{:S(2)}) async-start(f32[16,2,1,8,128]{4,3,1,2,0:T(8,128)} %bitcast.11), calls=%async_computation.3 | async-start | bytes 262144 | tf_op jit(solution)/shard_map/all_to_all | solution.py:124
Sparse Core Ops, SparseCore 0:
  18.7 74.6 all-gather.1
where the time goes:
time: 399 us; the launch traced here: 397 us
  waiting for transfers between devices  179 us (45%)
  matrix products  89.1 us (22%)
  other arithmetic  41.5 us (10%)
  starting transfers between devices  34.2 us (9%)
  local copies, waits for them, and re-layouts  29.3 us (7%)
  between operations  13.7 us (3%)
  blocking collectives  11.1 us (3%)
    all_to_all x1, waiting for transfers between devices, local(): lax.all_to_all(found[2][None], 'ctx', split_axis=1, concat_axis=0, tiled=...  84.4 us
    all_gather x1, waiting for transfers between devices, local(): lax.all_gather(local_rows, 'ctx', axis=0, tiled=True)  74.7 us
    dot_general x7, matrix products, block_part(): jnp.einsum(form, weights, values, preferred_element_type=jnp.float32)  51.1 us
    dot_general x4, matrix products, prompt_step(): jnp.einsum('rtgqd,kgd->rtgqk', grouped, blocks_pair[0], preferred_element...  36 us
    reduce_sum x7, other arithmetic, block_part(): block_total = jnp.sum(weights, axis=-1, dtype=jnp.float32)  35.7 us
    all_to_all x1, starting transfers between devices, local(): lax.all_to_all(mine[1], 'dec', split_axis=0, concat_axis=2, tiled=True)  11.9 us
    all_to_all x1, blocking collectives, local(): lax.all_to_all(by_group, 'dec', split_axis=2, concat_axis=0, tiled=True)  11.1 us
  transfers between devices with their start and end apart: 7, of which 6 were waited for; matrix products, arithmetic and copies ran while one was open for 6% of the time, Pallas kernels for 0%

commit v1 on v0

v1 whole, which is shorter than its diff:
```python
import functools
import math

import jax
import jax.numpy as jnp
from jax import lax
from jax.experimental import pallas as pl
from jax.experimental.pallas import tpu as pltpu
from jax.sharding import Mesh, PartitionSpec as P

MASKED_SCORE = -1e30
CODE_SPAN = 126.0
BF16 = jnp.bfloat16
F32 = jnp.float32


def dot_nt(a, b):
    return lax.dot_general(a, b, (((1,), (1,)), ((), ())), preferred_element_type=F32)


def split3(x):
    hi = x.astype(BF16).astype(F32)
    mid = (x - hi).astype(BF16).astype(F32)
    return hi, mid, x - hi - mid


def prompt_kernel(blocks, scale, carried, final, chunk, per_dest, *refs):
    q_ref = refs[0]
    k_refs = refs[1 : 1 + blocks]
    v_refs = refs[1 + blocks : 1 + 2 * blocks]
    rest = refs[1 + 2 * blocks :]
    if carried:
        acc_in, stat_in = rest[:2]
        rest = rest[2:]
    wide = rest[-1]
    rows, head_dim = q_ref.shape
    keys = k_refs[0].shape[0]

    @pl.when(pl.program_id(0) == 0)
    def _():
        for b in range(blocks):
            wide[b, :, :head_dim] = v_refs[b][...]
            wide[b, :, head_dim:] = jnp.ones((keys, head_dim), BF16)

    sub = 256
    for start in range(0, rows, sub):
        here = slice(start, start + sub)
        q = q_ref[here]
        if carried:
            acc = acc_in[here]
            top = stat_in[here, 0:1]
            total = jnp.broadcast_to(stat_in[here, 64:65], (sub, head_dim))
        else:
            acc = None
        for b in range(blocks):
            for offset in range(0, keys, chunk):
                scores = dot_nt(q, k_refs[b][offset : offset + chunk])
                part_top = jnp.max(scores, axis=1, keepdims=True)
                if acc is None:
                    new_top = part_top
                else:
                    new_top = jnp.maximum(top, part_top)
                    factor = jnp.exp2((top - new_top) * scale)
                weights = jnp.exp2((scores - new_top) * scale).astype(BF16)
                both = jnp.dot(weights, wide[b, offset : offset + chunk], preferred_element_type=F32)
                if acc is None:
                    acc, total = both[:, :head_dim], both[:, head_dim:]
                else:
                    acc = acc * factor + both[:, :head_dim]
                    total = total * factor + both[:, head_dim:]
                top = new_top
        lane = lax.broadcasted_iota(jnp.int32, (sub, head_dim), 1)
        if not final:
            acc_out, stat_out = rest[:2]
            acc_out[here] = acc
            stat_out[here] = jnp.where(lane < 64, jnp.broadcast_to(top, (sub, head_dim)), total)
        else:
            encode(rest[0], start // per_dest, sub // per_dest, per_dest, acc / total, top * scale + jnp.log2(total))


def encode(out_ref, first, count, per_dest, value, level):
    head_dim = value.shape[1]
    size = jnp.max(jnp.abs(value), axis=1, keepdims=True)
    size = jnp.maximum(size, 1e-30)
    size = size * (1.0 + 2.0**-20)
    coded = jnp.exp2(value * (CODE_SPAN / size)).astype(BF16)
    size = jnp.broadcast_to(size, value.shape)
    pieces = split3(level) + split3(size)
    lane = lax.broadcasted_iota(jnp.int32, (16, head_dim), 1)
    for i in range(count):
        base = i * per_dest
        out_ref[first + i, 0:per_dest, :] = coded[base : base + per_dest]
        packed = jnp.zeros((16, head_dim), F32)
        for half in range(per_dest // 16):
            for n, piece in enumerate(pieces):
                rows = piece[base + half * 16 : base + half * 16 + 16]
                packed = jnp.where(lane == half * 8 + n, rows, packed)
        out_ref[first + i, per_dest : per_dest + 16, :] = packed.astype(BF16)


def prompt_call(q, keys, values, carry, final, tile, chunk, scale, per_dest):
    rows, head_dim = q.shape
    positions = keys[0].shape[0]
    blocks = len(keys)
    row_spec = pl.BlockSpec((tile, head_dim), lambda i: (i, 0))
    full = pl.BlockSpec((positions, head_dim), lambda i: (0, 0))
    if final:
        dests = rows // per_dest
        out_specs = pl.BlockSpec((tile // per_dest, per_dest + 16, head_dim), lambda i: (i, 0, 0))
        out_shape = jax.ShapeDtypeStruct((dests, per_dest + 16, head_dim), BF16)
    else:
        out_specs = [row_spec, row_spec]
        out_shape = [jax.ShapeDtypeStruct((rows, head_dim), F32)] * 2
    carry = [] if carry is None else list(carry)
    work = rows * positions * blocks
    return pl.pallas_call(
        functools.partial(prompt_kernel, blocks, scale, bool(carry), final, chunk, per_dest),
        grid=(rows // tile,),
        in_specs=[row_spec] + [full] * (2 * blocks) + [row_spec] * len(carry),
        out_specs=out_specs,
        out_shape=out_shape,
        scratch_shapes=[pltpu.VMEM((blocks, positions, 2 * head_dim), BF16)],
        compiler_params=pltpu.CompilerParams(vmem_limit_bytes=48 << 20),
        cost_estimate=pl.CostEstimate(
            flops=4 * work * head_dim,
            bytes_accessed=4 * blocks * positions * head_dim + 6 * rows * head_dim,
            transcendentals=work,
        ),
        name="prompt",
    )(q, *keys, *values, *carry)


def suffix_kernel(scale, samples, groups, steps, q_ref, k_ref, v_ref, nk_ref, nv_ref, len_ref, out_ref, level_ref):
    sample = pl.program_id(0)
    per_sample = q_ref.shape[1] // samples
    head_dim = q_ref.shape[2]
    q = q_ref[:, pl.ds(pl.multiple_of(sample * per_sample, per_sample), per_sample), :]
    rows = groups * per_sample
    q = q.reshape(rows, head_dim)
    per_step = per_sample // steps
    length = len_ref[sample]
    flat = k_ref.shape[1]
    span = 2048

    def step(keys, values, visible, state):
        scores = jnp.where(visible, dot_nt(q, keys), MASKED_SCORE)
        part_top = jnp.max(scores, axis=1, keepdims=True)
        if state is None:
            new_top = part_top
        else:
            new_top = jnp.maximum(state[0], part_top)
        weights = jnp.exp2((scores - new_top) * scale)
        part_total = jnp.sum(weights, axis=1, keepdims=True)
        part = jnp.dot(weights.astype(BF16), values, preferred_element_type=F32)
        if state is None:
            return new_top, part_total, part
        factor = jnp.exp2((state[0] - new_top) * scale)
        return new_top, state[1] * factor + part_total, state[2] * factor + part

    def same_group(columns):
        row = lax.broadcasted_iota(jnp.int32, (rows, columns), 0)
        column = lax.broadcasted_iota(jnp.int32, (rows, columns), 1)
        return row, column, (row // per_sample) == (column % groups)

    new_count = nk_ref.shape[1]
    row, column, same = same_group(new_count)
    visible = same & (column // groups <= (row // per_step) % steps)
    state = step(nk_ref[0], nv_ref[0], visible, None)
    _, column, same = same_group(span)
    place = column // groups
    for offset in range(0, flat, span):
        visible = same & (place < length - offset // groups)
        state = step(k_ref[0, offset : offset + span], v_ref[0, offset : offset + span], visible, state)
    out_ref[0] = state[2] / state[1]
    level_ref[0] = jnp.broadcast_to(state[0] * scale + jnp.log2(state[1]), (rows, head_dim))


def suffix_call(q, keys, values, new_keys, new_values, lengths, scale, steps):
    groups, _, head_dim = q.shape
    samples, flat, _ = keys.shape
    new_count = new_keys.shape[1]
    rows = groups * q.shape[1] // samples
    cache = pl.BlockSpec((1, flat, head_dim), lambda s: (s, 0, 0))
    fresh = pl.BlockSpec((1, new_count, head_dim), lambda s: (s, 0, 0))
    out = pl.BlockSpec((1, rows, head_dim), lambda s: (s, 0, 0))
    return pl.pallas_call(
        functools.partial(suffix_kernel, scale, samples, groups, steps),
        grid=(samples,),
        in_specs=[
            pl.BlockSpec(q.shape, lambda s: (0, 0, 0)),
            cache,
            cache,
            fresh,
            fresh,
            pl.BlockSpec(memory_space=pltpu.SMEM),
        ],
        out_specs=[out, out],
        out_shape=[jax.ShapeDtypeStruct((samples, rows, head_dim), F32)] * 2,
        compiler_params=pltpu.CompilerParams(vmem_limit_bytes=48 << 20),
        cost_estimate=pl.CostEstimate(
            flops=4 * samples * rows * flat * head_dim,
            bytes_accessed=4 * samples * flat * head_dim,
            transcendentals=samples * rows * flat,
        ),
        name="suffix",
    )(q, keys, values, new_keys, new_values, lengths)


def merge_kernel(sources, groups, samples, steps, got_ref, own_ref, own_level_ref, out_ref):
    head_dim = own_ref.shape[2]
    per_sample = own_ref.shape[1] // groups
    per_step = per_sample // steps
    per_dest = samples * per_sample
    for g in range(groups):
        levels = [[] for _ in range(samples)]
        sizes = [[] for _ in range(samples)]
        for z in range(sources):
            packed = got_ref[z * groups + g, per_dest : per_dest + 16, :].astype(F32)
            for half in range(per_dest // 16):
                at = [
                    jnp.broadcast_to(packed[:, half * 8 + n : half * 8 + n + 1], (16, head_dim))
                    for n in range(6)
                ]
                levels[half].append(at[0] + at[1] + at[2])
                sizes[half].append((at[3] + at[4] + at[5]) * (1.0 / CODE_SPAN))
        for s in range(samples):
            own_level = own_level_ref[s, g * per_sample : (g + 1) * per_sample, :]
            highest = own_level
            for level in levels[s]:
                highest = jnp.maximum(highest, level)
            weight = jnp.exp2(own_level - highest)
            total = weight
            summed = weight * own_ref[s, g * per_sample : (g + 1) * per_sample, :]
            for z in range(sources):
                coded = got_ref[z * groups + g, s * per_sample : (s + 1) * per_sample, :].astype(F32)
                weight = jnp.exp2(levels[s][z] - highest)
                total = total + weight
                summed = summed + weight * (jnp.log2(coded) * sizes[s][z])
            result = summed / total
            for t in range(steps):
                out_ref[s * steps + t, g * per_step : (g + 1) * per_step, :] = result[
                    t * per_step : (t + 1) * per_step
                ]


def merge_call(got, own, own_level, sources, groups, steps):
    samples, rows, head_dim = own.shape
    heads = rows // steps
    return pl.pallas_call(
        functools.partial(merge_kernel, sources, groups, samples, steps),
        out_shape=jax.ShapeDtypeStruct((samples * steps, heads, head_dim), F32),
        compiler_params=pltpu.CompilerParams(vmem_limit_bytes=48 << 20),
        name="merge",
    )(got, own, own_level)


def local(x_size, z_size, dec_size, queries, prompt_keys, prompt_values, suffix_keys, suffix_values, new_keys, new_values, lengths):
    samples, steps, width = queries.shape
    _, suffix_length, groups, head_dim = suffix_keys.shape
    per_group = width // (groups * head_dim)
    scale = head_dim ** (-0.5) * math.log2(math.e)
    keys = prompt_keys.reshape(-1, head_dim)
    values = prompt_values.reshape(-1, head_dim)

    def shift(array, amount):
        return lax.ppermute(array, "x", [(i, (i + amount) % x_size) for i in range(x_size)])

    keys_left, values_left = shift(keys, 1), shift(values, 1)
    keys_right, values_right = shift(keys, -1), shift(values, -1)
    keys_far, values_far = shift(keys_left, 1), shift(values_right, -1)

    per_dest = samples * steps * per_group
    by_group = (
        queries.reshape(samples, steps, groups, per_group, head_dim)
        .transpose(2, 0, 1, 3, 4)
        .reshape(groups, per_dest, head_dim)
    )
    spread = jnp.broadcast_to(by_group[None], (z_size,) + by_group.shape).reshape(
        z_size * groups, per_dest, head_dim
    )
    rows = lax.all_to_all(spread, ("z", "dec"), 0, 0, tiled=True).reshape(-1, head_dim)

    own, own_level = suffix_call(
        by_group,
        suffix_keys.reshape(samples, suffix_length * groups, head_dim),
        suffix_values.reshape(samples, suffix_length * groups, head_dim),
        new_keys.reshape(samples, steps * groups, head_dim),
        new_values.reshape(samples, steps * groups, head_dim),
        lengths,
        scale,
        steps,
    )
    carry = prompt_call(rows, [keys], [values], None, False, 1024, 2048, scale, per_dest)
    coded = prompt_call(
        rows,
        [keys_left, keys_right, keys_far],
        [values_left, values_right, values_far],
        carry,
        True,
        512,
        2048,
        scale,
        per_dest,
    )
    got = lax.all_to_all(coded, ("z", "dec"), 0, 0, tiled=True)
    out = merge_call(got, own, own_level, z_size, groups, steps)
    return out.astype(BF16).reshape(samples, steps, width)


def solution(mesh):
    ctx_size, dec_size = mesh.devices.shape
    x_size = 4
    z_size = ctx_size // x_size
    split = Mesh(mesh.devices.reshape(x_size, z_size, dec_size), ("x", "z", "dec"))
    rows = ("x", "z", "dec")
    return jax.shard_map(
        functools.partial(local, x_size, z_size, dec_size),
        mesh=split,
        in_specs=(
            P(rows, None, None),
            P(("x", "z"), "dec", None),
            P(("x", "z"), "dec", None),
            P(rows, None, None, None),
            P(rows, None, None, None),
            P(rows, None, None, None),
            P(rows, None, None, None),
            P(rows),
        ),
        out_specs=P(rows, None, None),
        check_vma=False,
    )
```

time: 399 us -> 110 us (0.28)
  waiting for transfers between devices: 179 us -> 34.7 us
  matrix products: 89.1 us -> 0 us
  other arithmetic: 41.5 us -> 0.01 us
  Pallas kernels: 0 us -> 35.6 us
  local copies, waits for them, and re-layouts: 29.3 us -> 7.7 us
  between operations: 13.7 us -> 0.12 us
  blocking collectives: 11.1 us -> 0 us
    all_to_all x6 -> x2, waiting for transfers between devices: 104 us -> 14.5 us  [the longest x1 14 us: local(): got = lax.all_to_all(coded, ('z', 'dec'), 0, 0, tiled=True)]
    dot_general x14 -> x0, matrix products: 89.1 us -> none  [the longest x7 51.1 us: block_part(): jnp.einsum(form, weights, values, preferred_element_type=jnp.float32)]
    all_gather x1 -> x0, waiting for transfers between devices: 74.7 us -> none  [local(): lax.all_gather(local_rows, 'ctx', axis=0, tiled=True)]
    reduce_sum x9 -> x0, other arithmetic: 39.3 us -> none  [the longest x7 35.7 us: block_part(): block_total = jnp.sum(weights, axis=-1, dtype=jnp.float32)]
    pallas_call x0 -> x4, Pallas kernels: none -> 35.6 us  [the longest x2 27.7 us: prompt_call(): pl.pallas_call(functools.partial(prompt_kernel, blocks, scale, bool(carry...]
    ppermute x0 -> x6, waiting for transfers between devices: none -> 20.2 us  [shift(): lax.ppermute(array, 'x', [(i, (i + amount) % x_size) for i in range(x_siz...]
    all_to_all x1 -> x0, blocking collectives: 11.1 us -> none  [local(): lax.all_to_all(by_group, 'dec', split_axis=2, concat_axis=0, tiled=True)]
    all_to_all x6 -> x2, starting transfers between devices: 34.2 us -> 24.4 us  [the longest x1 13.2 us: local(): lax.all_to_all(spread, ('z', 'dec'), 0, 0, tiled=True).reshape(-1, head_dim)]
  transfers between devices with their start and end apart: 7 -> 8, of which waited for: 6 -> 4; matrix products, arithmetic and copies ran while one was open for 6% -> 0% of each run, Pallas kernels for 0% -> 12%
where the time goes in v1:
time: 110 us; the launch traced here: 109 us
  Pallas kernels  35.6 us (32%)
  waiting for transfers between devices  34.7 us (32%)
  starting transfers between devices  31.3 us (28%)
  local copies, waits for them, and re-layouts  7.7 us (7%)
    pallas_call x2, Pallas kernels, prompt_call(): pl.pallas_call(functools.partial(prompt_kernel, blocks, scale, bool(carry...  27.7 us
    ppermute x6, waiting for transfers between devices, shift(): lax.ppermute(array, 'x', [(i, (i + amount) % x_size) for i in range(x_siz...  20.2 us
    all_to_all x1, waiting for transfers between devices, local(): got = lax.all_to_all(coded, ('z', 'dec'), 0, 0, tiled=True)  14 us
    all_to_all x1, starting transfers between devices, local(): lax.all_to_all(spread, ('z', 'dec'), 0, 0, tiled=True).reshape(-1, head_dim)  13.2 us
    all_to_all x1, starting transfers between devices, local(): got = lax.all_to_all(coded, ('z', 'dec'), 0, 0, tiled=True)  11.2 us
    ppermute x6, starting transfers between devices, shift(): lax.ppermute(array, 'x', [(i, (i + amount) % x_size) for i in range(x_siz...  6.9 us
    pallas_call x1, Pallas kernels, suffix_call(): pl.pallas_call(functools.partial(suffix_kernel, scale, samples, groups, s...  6.47 us
    unnamed x14, local copies, waits for them, and re-layouts  5.25 us
  transfers between devices with their start and end apart: 8, of which 4 were waited for; matrix products, arithmetic and copies ran while one was open for 0% of the time, Pallas kernels for 12%

profile of v1, /device:TPU:1, one launch (start us, length us, event | category | flops | bytes accessed | tf_op | source)
XLA Modules:
  0.0 109.5 jit_solution(18204926994958020096)
XLA Ops:
  0.0 0.9 reshape.32
  0.9 0.9 broadcast_in_dim.8
  1.8 13.2 %all-to-all-start = ((bf16[64,32,128]{2,1,0:T(8,128)(2,1)}), bf16[64,32,128]{2,1,0:T(8,128)(2,1)S(1)}, u32[]{:S(2)}, u32[]{:S(2)}) async-start(bf16[64,32,128]{2,1,0:T(8,128)(2,1)} %bitcast.2), calls=%async_computation | async-start | bytes 1048576 | tf_op jit(solution)/shard_map/all_to_all | solution.py:281
  15.0 1.3 %collective-permute-start = (bf16[2048,128]{1,0:T(8,128)(2,1)}, bf16[2048,128]{1,0:T(8,128)(2,1)S(1)}, u32[]{:S(2)}, u32[]{:S(2)}) collective-permute-start(bf16[2048,128]{1,0:T(8,128)(2,1)} %bitcast.18), channel_id=1, source_target_pairs={{0,64},{64,128},{128,192},{192,0},{1,65},{65,129},{129,193},{193,1... | collective-permute-start | bytes 1572872 | tf_op jit(solution)/shard_map/ppermute | solution.py:266
  16.3 1.5 %collective-permute-start.4 = (bf16[2048,128]{1,0:T(8,128)(2,1)}, bf16[2048,128]{1,0:T(8,128)(2,1)S(1)}, u32[]{:S(2)}, u32[]{:S(2)}) collective-permute-start(bf16[2048,128]{1,0:T(8,128)(2,1)} %bitcast.21), channel_id=1, source_target_pairs={{0,192},{64,0},{128,64},{192,128},{1,193},{65,1},{129,65},{193,129... | collective-permute-start | bytes 1572872 | tf_op jit(solution)/shard_map/ppermute | solution.py:266
  17.7 1.3 %collective-permute-start.1 = (bf16[2048,128]{1,0:T(8,128)(2,1)}, bf16[2048,128]{1,0:T(8,128)(2,1)S(1)}, u32[]{:S(2)}, u32[]{:S(2)}) collective-permute-start(bf16[2048,128]{1,0:T(8,128)(2,1)} %bitcast.19), channel_id=1, source_target_pairs={{0,192},{64,0},{128,64},{192,128},{1,193},{65,1},{129,65},{193,129... | collective-permute-start | bytes 1572872 | tf_op jit(solution)/shard_map/ppermute | solution.py:266
  19.0 0.2 collective-permute-start.3
  19.2 10.3 %collective-permute-done.refs_1_ = bf16[2048,128]{1,0:T(8,128)(2,1)S(1)} collective-permute-done((bf16[2048,128]{1,0:T(8,128)(2,1)}, bf16[2048,128]{1,0:T(8,128)(2,1)S(1)}, u32[]{:S(2)}, u32[]{:S(2)}) %collective-permute-start) | collective-permute-done | bytes 524320 | tf_op jit(solution)/shard_map/ppermute | solution.py:266
  29.5 0.0 collective-permute-start.2
  29.5 0.0 collective-permute-done.4.refs_5_
  29.5 2.7 %collective-permute-start.5 = (bf16[2048,128]{1,0:T(8,128)(2,1)S(1)}, bf16[2048,128]{1,0:T(8,128)(2,1)}, u32[]{:S(2)}, u32[]{:S(2)}) collective-permute-start(bf16[2048,128]{1,0:T(8,128)(2,1)S(1)} %collective-permute-done.4.refs_5_), channel_id=1, source_target_pairs={{0,192},{64,0},{128,64},{192,128},{1,193},{65,1},{129,65},{193,129... | collective-permute-start | bytes 1572872 | tf_op jit(solution)/shard_map/ppermute | solution.py:266
  32.2 0.5 all-to-all-done
  32.7 0.0 copy-start.4
  32.7 1.0 copy-done.4
  33.7 0.0 copy-start.5
  33.7 1.0 copy-done.5
  34.8 6.4 %prompt.2 = (f32[2048,128]{1,0:T(8,128)S(1)}, f32[2048,128]{1,0:T(8,128)S(1)}) custom-call(bf16[2048,128]{1,0:T(8,128)(2,1)S(1)} %bitcast.14, bf16[2048,128]{1,0:T(8,128)(2,1)S(1)} %bitcast.20, bf16[2048,128]{1,0:T(8,128)(2,1)S(1)} %bitcast.23), custom_call_target="tpu_custom_call" | custom-call | flops 2147483648 | bytes 2621440 | tf_op jit(solution)/shard_map/prompt/pallas_call | solution.py:116
  41.2 0.0 copy-start.6
  41.2 1.0 copy-done.6
  42.2 0.0 collective-permute-done.1.refs_2_
  42.2 0.0 collective-permute-done.3.refs_4_
  42.2 9.9 %collective-permute-done.2.refs_3_ = bf16[2048,128]{1,0:T(8,128)(2,1)} collective-permute-done((bf16[2048,128]{1,0:T(8,128)(2,1)S(1)}, bf16[2048,128]{1,0:T(8,128)(2,1)}, u32[]{:S(2)}, u32[]{:S(2)}) %collective-permute-start.2) | collective-permute-done | bytes 524320 | tf_op jit(solution)/shard_map/ppermute | solution.py:266
  52.1 0.0 collective-permute-done.5.refs_6_
  52.1 0.0 copy-start.1
  52.1 0.0 copy-start.2
  52.1 0.0 copy-start.3
  52.1 21.3 %prompt.3 = bf16[64,48,128]{2,1,0:T(8,128)(2,1)} custom-call(bf16[2048,128]{1,0:T(8,128)(2,1)S(1)} %bitcast.15, bf16[2048,128]{1,0:T(8,128)(2,1)S(1)} %collective-permute-done.refs_1_, bf16[2048,128]{1,0:T(8,128)(2,1)S(1)} %collective-permute-done.1.refs_2_, bf16[2048,128]{1,0:T(8,128)(2,1)} %collective-permute-done.2.refs_3_, ...), custom_call_target="tpu_custom_call" | custom-call | flops 6442450944 | bytes 4718592 | tf_op jit(solution)/shard_map/prompt/pallas_call | solution.py:116
  73.4 11.2 %all-to-all-start.1 = ((bf16[64,48,128]{2,1,0:T(8,128)(2,1)}), bf16[64,48,128]{2,1,0:T(8,128)(2,1)S(1)}, u32[]{:S(2)}, u32[]{:S(2)}) async-start(bf16[64,48,128]{2,1,0:T(8,128)(2,1)} %prompt.3), calls=%async_computation.1 | async-start | bytes 1572864 | tf_op jit(solution)/shard_map/all_to_all | solution.py:305
  84.6 0.0 copy-done.1
  84.6 0.0 copy-done.2
  84.6 0.0 copy-done.3
  84.6 0.0 copy-start
  84.7 2.2 %copy-done = bf16[2,1024,8,128]{3,2,1,0:T(8,128)(2,1)S(1)} copy-done((bf16[2,1024,8,128]{3,2,1,0:T(8,128)(2,1)S(1)}, bf16[2,1024,8,128]{3,2,1,0:T(8,128)(2,1)}, u32[]{:S(2)}) %copy-start) | copy-done | bytes 4194328
  86.8 6.5 %suffix.1 = (f32[2,128,128]{2,1,0:T(8,128)S(1)}, f32[2,128,128]{2,1,0:T(8,128)S(1)}) custom-call(bf16[8,32,128]{2,1,0:T(8,128)(2,1)S(1)} %bitcast.13, bf16[2,8192,128]{2,1,0:T(8,128)(2,1)S(1)} %bitcast.11, bf16[2,8192,128]{2,1,0:T(8,128)(2,1)} %bitcast.24, bf16[2,16,128]{2,1,0:T(8,128)(2,1)S(1)} %bitcast.16, bf16[2,16,128]{2,1,0:T(8,128)(2,1)S(1)} %bitcast.17, ...), custom_call_target="tpu_custom_call" | custom-call | flops 1073741824 | bytes 8388608 | tf_op jit(solution)/shard_map/suffix/pallas_call | solution.py:186
  93.3 14.0 %all-to-all-done.1.got_ref = bf16[64,48,128]{2,1,0:T(8,128)(2,1)S(1)} async-done(((bf16[64,48,128]{2,1,0:T(8,128)(2,1)}), bf16[64,48,128]{2,1,0:T(8,128)(2,1)S(1)}, u32[]{:S(2)}, u32[]{:S(2)}) %all-to-all-start.1) | async-done | bytes 786464 | tf_op jit(solution)/shard_map/all_to_all | solution.py:305
  107.4 1.4 %merge.1 = f32[4,64,128]{2,1,0:T(8,128)S(1)} custom-call(bf16[64,48,128]{2,1,0:T(8,128)(2,1)S(1)} %all-to-all-done.1.got_ref, f32[2,128,128]{2,1,0:T(8,128)S(1)} %get-tuple-element.11.own_ref, f32[2,128,128]{2,1,0:T(8,128)S(1)} %get-tuple-element.12.own_level_ref), custom_call_target="tpu_custom_call" | custom-call | tf_op jit(solution)/shard_map/merge/pallas_call | solution.py:249
  108.8 0.6 reshape.41
  (2 shorter events, 0.0 us)
Async XLA Ops:
  1.8 30.9 %all-to-all-start = ((bf16[64,32,128]{2,1,0:T(8,128)(2,1)}), bf16[64,32,128]{2,1,0:T(8,128)(2,1)S(1)}, u32[]{:S(2)}, u32[]{:S(2)}) async-start(bf16[64,32,128]{2,1,0:T(8,128)(2,1)} %bitcast.2), calls=%async_computation | async-start | bytes 1048576 | tf_op jit(solution)/shard_map/all_to_all | solution.py:281
  15.0 14.5 %collective-permute-start = (bf16[2048,128]{1,0:T(8,128)(2,1)}, bf16[2048,128]{1,0:T(8,128)(2,1)S(1)}, u32[]{:S(2)}, u32[]{:S(2)}) collective-permute-start(bf16[2048,128]{1,0:T(8,128)(2,1)} %bitcast.18), channel_id=1, source_target_pairs={{0,64},{64,128},{128,192},{192,0},{1,65},{65,129},{129,193},{193,1... | collective-permute-start | bytes 1572872 | tf_op jit(solution)/shard_map/ppermute | solution.py:266
  16.3 13.3 %collective-permute-start.4 = (bf16[2048,128]{1,0:T(8,128)(2,1)}, bf16[2048,128]{1,0:T(8,128)(2,1)S(1)}, u32[]{:S(2)}, u32[]{:S(2)}) collective-permute-start(bf16[2048,128]{1,0:T(8,128)(2,1)} %bitcast.21), channel_id=1, source_target_pairs={{0,192},{64,0},{128,64},{192,128},{1,193},{65,1},{129,65},{193,129... | collective-permute-start | bytes 1572872 | tf_op jit(solution)/shard_map/ppermute | solution.py:266
  17.7 24.5 %collective-permute-start.1 = (bf16[2048,128]{1,0:T(8,128)(2,1)}, bf16[2048,128]{1,0:T(8,128)(2,1)S(1)}, u32[]{:S(2)}, u32[]{:S(2)}) collective-permute-start(bf16[2048,128]{1,0:T(8,128)(2,1)} %bitcast.19), channel_id=1, source_target_pairs={{0,192},{64,0},{128,64},{192,128},{1,193},{65,1},{129,65},{193,129... | collective-permute-start | bytes 1572872 | tf_op jit(solution)/shard_map/ppermute | solution.py:266
  19.0 23.2 %collective-permute-start.3 = (bf16[2048,128]{1,0:T(8,128)(2,1)}, bf16[2048,128]{1,0:T(8,128)(2,1)S(1)}, u32[]{:S(2)}, u32[]{:S(2)}) collective-permute-start(bf16[2048,128]{1,0:T(8,128)(2,1)} %bitcast.22), channel_id=1, source_target_pairs={{0,64},{64,128},{128,192},{192,0},{1,65},{65,129},{129,193},{193,1... | collective-permute-start | bytes 1572872 | tf_op jit(solution)/shard_map/ppermute | solution.py:266
  29.5 22.6 %collective-permute-start.2 = (bf16[2048,128]{1,0:T(8,128)(2,1)S(1)}, bf16[2048,128]{1,0:T(8,128)(2,1)}, u32[]{:S(2)}, u32[]{:S(2)}) collective-permute-start(bf16[2048,128]{1,0:T(8,128)(2,1)S(1)} %collective-permute-done.refs_1_), channel_id=1, source_target_pairs={{0,64},{64,128},{128,192},{192,0},{1,65},{65,129},{129,193},{193,1... | collective-permute-start | bytes 1572872 | tf_op jit(solution)/shard_map/ppermute | solution.py:266
  29.5 22.6 %collective-permute-start.5 = (bf16[2048,128]{1,0:T(8,128)(2,1)S(1)}, bf16[2048,128]{1,0:T(8,128)(2,1)}, u32[]{:S(2)}, u32[]{:S(2)}) collective-permute-start(bf16[2048,128]{1,0:T(8,128)(2,1)S(1)} %collective-permute-done.4.refs_5_), channel_id=1, source_target_pairs={{0,192},{64,0},{128,64},{192,128},{1,193},{65,1},{129,65},{193,129... | collective-permute-start | bytes 1572872 | tf_op jit(solution)/shard_map/ppermute | solution.py:266
  32.7 1.0 copy-start.4
  33.7 1.0 copy-start.5
  41.2 1.0 copy-start.6
  52.1 32.5 %copy-start.1 = (bf16[2,2,8,128]{3,2,1,0:T(8,128)(2,1)S(1)}, bf16[2,2,8,128]{3,2,1,0:T(8,128)(2,1)}, u32[]{:S(2)}) copy-start(bf16[2,2,8,128]{3,2,1,0:T(8,128)(2,1)} %param.13) | copy-start | bytes 24580
  52.1 32.5 %copy-start.2 = (bf16[2,2,8,128]{3,2,1,0:T(8,128)(2,1)S(1)}, bf16[2,2,8,128]{3,2,1,0:T(8,128)(2,1)}, u32[]{:S(2)}) copy-start(bf16[2,2,8,128]{3,2,1,0:T(8,128)(2,1)} %param.14) | copy-start | bytes 24580
  52.1 32.5 %copy-start.3 = (s32[2]{0:T(128)S(1)}, s32[2]{0:T(128)}, u32[]{:S(2)}) copy-start(s32[2]{0:T(128)} %len_ref.1) | copy-start | bytes 28
  73.4 34.0 %all-to-all-start.1 = ((bf16[64,48,128]{2,1,0:T(8,128)(2,1)}), bf16[64,48,128]{2,1,0:T(8,128)(2,1)S(1)}, u32[]{:S(2)}, u32[]{:S(2)}) async-start(bf16[64,48,128]{2,1,0:T(8,128)(2,1)} %prompt.3), calls=%async_computation.1 | async-start | bytes 1572864 | tf_op jit(solution)/shard_map/all_to_all | solution.py:305
  84.6 2.2 %copy-start = (bf16[2,1024,8,128]{3,2,1,0:T(8,128)(2,1)S(1)}, bf16[2,1024,8,128]{3,2,1,0:T(8,128)(2,1)}, u32[]{:S(2)}) copy-start(bf16[2,1024,8,128]{3,2,1,0:T(8,128)(2,1)} %param.11) | copy-start | bytes 12582916

commit v2 on v1

v2 whole, which is shorter than its diff:
```python
import functools
import math

import jax
import jax.numpy as jnp
from jax import lax
from jax.experimental import pallas as pl
from jax.experimental.pallas import tpu as pltpu
from jax.sharding import Mesh, PartitionSpec as P

MASKED_SCORE = -1e30
CODE_SPAN = 126.0
STAT_ROWS = 8
VMEM_BYTES = 32 << 20
BF16 = jnp.bfloat16
F32 = jnp.float32


def dot_nt(a, b):
    return lax.dot_general(a, b, (((1,), (1,)), ((), ())), preferred_element_type=F32)


def split3(x):
    hi = x.astype(BF16).astype(F32)
    mid = (x - hi).astype(BF16).astype(F32)
    return hi, mid, x - hi - mid


def prompt_kernel(blocks, scale, carried, final, sub, chunk, per_dest, *refs):
    q_ref = refs[0]
    k_refs = refs[1 : 1 + blocks]
    v_refs = refs[1 + blocks : 1 + 2 * blocks]
    rest = refs[1 + 2 * blocks :]
    if carried:
        acc_in, stat_in = rest[:2]
        rest = rest[2:]
    rows, head_dim = q_ref.shape
    keys = k_refs[0].shape[0]
    items = [
        (start, b, offset)
        for start in range(0, rows, sub)
        for b in range(blocks)
        for offset in range(0, keys, chunk)
    ]

    def score(item):
        start, b, offset = item
        return dot_nt(q_ref[start : start + sub], k_refs[b][offset : offset + chunk])

    def finish(start, acc, top, total):
        if final:
            encode(rest[0], start // per_dest, sub // per_dest, per_dest, acc / total, top * scale + jnp.log2(total))
        else:
            lane = lax.broadcasted_iota(jnp.int32, (sub, head_dim), 1)
            rest[0][start : start + sub] = acc
            rest[1][start : start + sub] = jnp.where(lane < 64, top, total)

    waiting = None
    ahead = score(items[0])
    for n, (start, b, offset) in enumerate(items):
        scores = ahead
        if n + 1 < len(items):
            ahead = score(items[n + 1])
        here = slice(start, start + sub)
        fresh = b == 0 and offset == 0
        if fresh and carried:
            acc = acc_in[here]
            top = stat_in[here, 0:1]
            total = stat_in[here, 64:65]
        elif fresh:
            acc = None
        part_top = jnp.max(scores, axis=1, keepdims=True)
        new_top = part_top if acc is None else jnp.maximum(top, part_top)
        weights = jnp.exp2((scores - new_top) * scale)
        part_total = jnp.sum(weights, axis=1, keepdims=True)
        part = jnp.dot(weights.astype(BF16), v_refs[b][offset : offset + chunk], preferred_element_type=F32)
        if acc is None:
            acc, total = part, part_total
        else:
            factor = jnp.exp2((top - new_top) * scale)
            acc = acc * factor + part
            total = total * factor + part_total
        top = new_top
        if waiting is not None:
            finish(*waiting)
            waiting = None
        if b == blocks - 1 and offset + chunk == keys:
            waiting = (start, acc, top, total)
    finish(*waiting)


def encode(out_ref, first, count, per_dest, value, level):
    head_dim = value.shape[1]
    size = jnp.maximum(jnp.max(jnp.abs(value), axis=1, keepdims=True), 1e-30)
    size = jnp.broadcast_to((size * (1.0 + 2.0**-7)).astype(BF16).astype(F32), value.shape)
    coded = jnp.exp2(value * (CODE_SPAN / size)).astype(BF16)
    pieces = split3(jnp.broadcast_to(level, value.shape)) + (size,)
    lane = lax.broadcasted_iota(jnp.int32, (STAT_ROWS, head_dim), 1)
    for i in range(count):
        base = i * per_dest
        out_ref[first + i, 0:per_dest, :] = coded[base : base + per_dest]
        packed = jnp.zeros((STAT_ROWS, head_dim), F32)
        for part in range(per_dest // STAT_ROWS):
            for n, piece in enumerate(pieces):
                at = base + part * STAT_ROWS
                packed = jnp.where(lane == part * 8 + n, piece[at : at + STAT_ROWS], packed)
        out_ref[first + i, per_dest : per_dest + STAT_ROWS, :] = packed.astype(BF16)


def prompt_call(q, keys, values, carry, final, tile, sub, chunk, scale, per_dest):
    rows, head_dim = q.shape
    positions = keys[0].shape[0]
    blocks = len(keys)
    row_spec = pl.BlockSpec((tile, head_dim), lambda i: (i, 0))
    full = pl.BlockSpec((positions, head_dim), lambda i: (0, 0))
    if final:
        dests = rows // per_dest
        out_specs = pl.BlockSpec((tile // per_dest, per_dest + STAT_ROWS, head_dim), lambda i: (i, 0, 0))
        out_shape = jax.ShapeDtypeStruct((dests, per_dest + STAT_ROWS, head_dim), BF16)
    else:
        out_specs = [row_spec, row_spec]
        out_shape = [jax.ShapeDtypeStruct((rows, head_dim), F32)] * 2
    carry = [] if carry is None else list(carry)
    work = rows * positions * blocks
    return pl.pallas_call(
        functools.partial(prompt_kernel, blocks, scale, bool(carry), final, sub, chunk, per_dest),
        grid=(rows // tile,),
        in_specs=[row_spec] + [full] * (2 * blocks) + [row_spec] * len(carry),
        out_specs=out_specs,
        out_shape=out_shape,
        compiler_params=pltpu.CompilerParams(vmem_limit_bytes=VMEM_BYTES),
        cost_estimate=pl.CostEstimate(
            flops=4 * work * head_dim,
            bytes_accessed=4 * blocks * positions * head_dim + 6 * rows * head_dim,
            transcendentals=work,
        ),
        name="prompt",
    )(q, *keys, *values, *carry)


def suffix_kernel(scale, groups, steps, q_ref, k_ref, v_ref, nk_ref, nv_ref, len_ref, out_ref, level_ref):
    q = q_ref[0]
    rows, head_dim = q.shape
    per_sample = rows // groups
    length = len_ref[pl.program_id(0)]
    flat = k_ref.shape[1]
    span = 2048

    def step(keys, values, visible, state):
        scores = jnp.where(visible, dot_nt(q, keys), MASKED_SCORE)
        part_top = jnp.max(scores, axis=1, keepdims=True)
        if state is None:
            new_top = part_top
        else:
            new_top = jnp.maximum(state[0], part_top)
        weights = jnp.exp2((scores - new_top) * scale)
        part_total = jnp.sum(weights, axis=1, keepdims=True)
        part = jnp.dot(weights.astype(BF16), values, preferred_element_type=F32)
        if state is None:
            return new_top, part_total, part
        factor = jnp.exp2((state[0] - new_top) * scale)
        return new_top, state[1] * factor + part_total, state[2] * factor + part

    def same_group(columns):
        row = lax.broadcasted_iota(jnp.int32, (rows, columns), 0)
        column = lax.broadcasted_iota(jnp.int32, (rows, columns), 1)
        return row, column, (row // per_sample) == (column % groups)

    new_count = nk_ref.shape[1]
    row, column, same = same_group(new_count)
    visible = same & (column // groups <= row % steps)
    state = step(nk_ref[0], nv_ref[0], visible, None)
    _, column, same = same_group(span)
    place = column // groups
    for offset in range(0, flat, span):
        visible = same & (place < length - offset // groups)
        state = step(k_ref[0, offset : offset + span], v_ref[0, offset : offset + span], visible, state)
    out_ref[0] = state[2] / state[1]
    level_ref[0] = jnp.broadcast_to(state[0] * scale + jnp.log2(state[1]), (rows, head_dim))


def suffix_call(q, keys, values, new_keys, new_values, lengths, scale, groups, steps):
    samples, rows, head_dim = q.shape
    flat = keys.shape[1]
    new_count = new_keys.shape[1]
    cache = pl.BlockSpec((1, flat, head_dim), lambda s: (s, 0, 0))
    fresh = pl.BlockSpec((1, new_count, head_dim), lambda s: (s, 0, 0))
    out = pl.BlockSpec((1, rows, head_dim), lambda s: (s, 0, 0))
    return pl.pallas_call(
        functools.partial(suffix_kernel, scale, groups, steps),
        grid=(samples,),
        in_specs=[
            out,
            cache,
            cache,
            fresh,
            fresh,
            pl.BlockSpec(memory_space=pltpu.SMEM),
        ],
        out_specs=[out, out],
        out_shape=[jax.ShapeDtypeStruct((samples, rows, head_dim), F32)] * 2,
        compiler_params=pltpu.CompilerParams(vmem_limit_bytes=VMEM_BYTES),
        cost_estimate=pl.CostEstimate(
            flops=4 * samples * rows * flat * head_dim,
            bytes_accessed=4 * samples * flat * head_dim,
            transcendentals=samples * rows * flat,
        ),
        name="suffix",
    )(q, keys, values, new_keys, new_values, lengths)


def merge_kernel(sources, groups, samples, got_ref, own_ref, own_level_ref, out_ref):
    head_dim = own_ref.shape[2]
    per_sample = own_ref.shape[1] // groups
    per_dest = samples * per_sample
    for g in range(groups):
        levels, sizes = [], []
        for z in range(sources):
            packed = got_ref[z * groups + g, per_dest : per_dest + STAT_ROWS, :].astype(F32)
            parts = [[], []]
            for part in range(per_dest // STAT_ROWS):
                at = [
                    jnp.broadcast_to(packed[:, part * 8 + n : part * 8 + n + 1], (STAT_ROWS, head_dim))
                    for n in range(4)
                ]
                parts[0].append(at[0] + at[1] + at[2])
                parts[1].append(at[3] * (1.0 / CODE_SPAN))
            levels.append(jnp.concatenate(parts[0], axis=0))
            sizes.append(jnp.concatenate(parts[1], axis=0))
        for s in range(samples):
            own_level = own_level_ref[s, g * per_sample : (g + 1) * per_sample, :]
            highest = own_level
            here = slice(s * per_sample, (s + 1) * per_sample)
            for level in levels:
                highest = jnp.maximum(highest, level[here])
            weight = jnp.exp2(own_level - highest)
            total = weight
            summed = weight * own_ref[s, g * per_sample : (g + 1) * per_sample, :]
            for z in range(sources):
                coded = got_ref[z * groups + g, here, :].astype(F32)
                weight = jnp.exp2(levels[z][here] - highest)
                total = total + weight
                summed = summed + weight * (jnp.log2(coded) * sizes[z][here])
            result = summed / total
            out_ref[s, g * per_sample : (g + 1) * per_sample, :] = result.astype(BF16)


def merge_call(got, own, own_level, sources, groups):
    return pl.pallas_call(
        functools.partial(merge_kernel, sources, groups, own.shape[0]),
        out_shape=jax.ShapeDtypeStruct(own.shape, BF16),
        compiler_params=pltpu.CompilerParams(vmem_limit_bytes=VMEM_BYTES),
        name="merge",
    )(got, own, own_level)


def local(x_size, z_size, dec_size, queries, prompt_keys, prompt_values, suffix_keys, suffix_values, new_keys, new_values, lengths):
    samples, steps, width = queries.shape
    _, suffix_length, groups, head_dim = suffix_keys.shape
    per_group = width // (groups * head_dim)
    scale = head_dim ** (-0.5) * math.log2(math.e)
    keys = prompt_keys.reshape(-1, head_dim)
    values = prompt_values.reshape(-1, head_dim)

    def shift(array, amount):
        return lax.ppermute(array, "x", [(i, (i + amount) % x_size) for i in range(x_size)])

    keys_left, values_left = shift(keys, 1), shift(values, 1)
    keys_right, values_right = shift(keys, -1), shift(values, -1)
    keys_far, values_far = shift(keys_left, 1), shift(values_right, -1)

    per_dest = samples * steps * per_group
    per_sample = (
        queries.reshape(samples, steps, groups * per_group, head_dim)
        .transpose(0, 2, 1, 3)
        .reshape(samples, groups, per_group * steps, head_dim)
    )
    spread = jnp.broadcast_to(
        per_sample.transpose(1, 0, 2, 3)[None], (z_size, groups, samples, per_group * steps, head_dim)
    ).reshape(z_size * groups, per_dest, head_dim)
    rows = lax.all_to_all(spread, ("z", "dec"), 0, 0, tiled=True).reshape(-1, head_dim)

    own, own_level = suffix_call(
        per_sample.reshape(samples, groups * per_group * steps, head_dim),
        suffix_keys.reshape(samples, suffix_length * groups, head_dim),
        suffix_values.reshape(samples, suffix_length * groups, head_dim),
        new_keys.reshape(samples, steps * groups, head_dim),
        new_values.reshape(samples, steps * groups, head_dim),
        lengths,
        scale,
        groups,
        steps,
    )
    def prompt(some_keys, some_values, carry, final):
        sub = 128 if final else 256
        return prompt_call(rows, some_keys, some_values, carry, final, 1024, sub, 2048, scale, per_dest)

    carry = prompt([keys], [values], None, False)
    carry = prompt([keys_left, keys_right], [values_left, values_right], carry, False)
    coded = prompt([keys_far], [values_far], carry, True)
    got = lax.all_to_all(coded, ("z", "dec"), 0, 0, tiled=True)
    out = merge_call(got, own, own_level, z_size, groups)
    return (
        out.reshape(samples, groups * per_group, steps, head_dim)
        .transpose(0, 2, 1, 3)
        .reshape(samples, steps, width)
    )


def solution(mesh):
    ctx_size, dec_size = mesh.devices.shape
    x_size = 4
    z_size = ctx_size // x_size
    split = Mesh(mesh.devices.reshape(x_size, z_size, dec_size), ("x", "z", "dec"))
    rows = ("x", "z", "dec")
    return jax.shard_map(
        functools.partial(local, x_size, z_size, dec_size),
        mesh=split,
        in_specs=(
            P(rows, None, None),
            P(("x", "z"), "dec", None),
            P(("x", "z"), "dec", None),
            P(rows, None, None, None),
            P(rows, None, None, None),
            P(rows, None, None, None),
            P(rows, None, None, None),
            P(rows),
        ),
        out_specs=P(rows, None, None),
        check_vma=False,
    )
```

time: 110 us -> 96.9 us (0.88)
  waiting for transfers between devices: 34.7 us -> 21.6 us
  Pallas kernels: 35.6 us -> 34.2 us
    ppermute x6, waiting for transfers between devices: 20.2 us -> 10.6 us  [shift(): lax.ppermute(array, 'x', [(i, (i + amount) % x_size) for i in range(x_siz...]
    all_to_all x1, waiting for transfers between devices: 14 us -> 10.5 us  [local(): got = lax.all_to_all(coded, ('z', 'dec'), 0, 0, tiled=True)]
    reshape x3 -> x0, local copies, waits for them, and re-layouts: 1.56 us -> none  [the longest x2 0.91 us: local(): queries.reshape(samples, steps, groups, per_group, head_dim)]
    unnamed x14 -> x16, local copies, waits for them, and re-layouts: 5.25 us -> 6.48 us
    pallas_call x2 -> x3, Pallas kernels: 27.7 us -> 27.1 us  [prompt_call(): pl.pallas_call(functools.partial(prompt_kernel, blocks, scale, bool(carry...]
  transfers between devices with their start and end apart: 8 -> 8, of which waited for: 4 -> 4; matrix products, arithmetic and copies ran while one was open for 0% -> 0% of each run, Pallas kernels for 12% -> 25%
where the time goes in v2:
time: 96.9 us; the launch traced here: 96.4 us
  Pallas kernels  34.2 us (35%)
  starting transfers between devices  32.3 us (33%)
  waiting for transfers between devices  21.6 us (22%)
  local copies, waits for them, and re-layouts  8.2 us (8%)
    pallas_call x3, Pallas kernels, prompt_call(): pl.pallas_call(functools.partial(prompt_kernel, blocks, scale, bool(carry...  27.1 us
    all_to_all x1, starting transfers between devices, local(): lax.all_to_all(spread, ('z', 'dec'), 0, 0, tiled=True).reshape(-1, head_dim)  13.2 us
    all_to_all x1, starting transfers between devices, local(): got = lax.all_to_all(coded, ('z', 'dec'), 0, 0, tiled=True)  12.2 us
    ppermute x6, waiting for transfers between devices, shift(): lax.ppermute(array, 'x', [(i, (i + amount) % x_size) for i in range(x_siz...  10.6 us
    all_to_all x1, waiting for transfers between devices, local(): got = lax.all_to_all(coded, ('z', 'dec'), 0, 0, tiled=True)  10.5 us
    ppermute x6, starting transfers between devices, shift(): lax.ppermute(array, 'x', [(i, (i + amount) % x_size) for i in range(x_siz...  6.9 us
    unnamed x16, local copies, waits for them, and re-layouts  6.48 us
    pallas_call x1, Pallas kernels, suffix_call(): pl.pallas_call(functools.partial(suffix_kernel, scale, groups, steps), gr...  5.4 us
  transfers between devices with their start and end apart: 8, of which 4 were waited for; matrix products, arithmetic and copies ran while one was open for 0% of the time, Pallas kernels for 25%

profile of v2, /device:TPU:1, one launch (start us, length us, event | category | flops | bytes accessed | tf_op | source)
XLA Modules:
  0.0 96.4 jit_solution(15270125272533924803)
XLA Ops:
  0.0 0.8 copy.10
  0.8 0.9 broadcast_in_dim.2
  1.7 13.2 %all-to-all-start = ((bf16[64,32,128]{2,1,0:T(8,128)(2,1)}), bf16[64,32,128]{2,1,0:T(8,128)(2,1)S(1)}, u32[]{:S(2)}, u32[]{:S(2)}) async-start(bf16[64,32,128]{2,1,0:T(8,128)(2,1)} %bitcast.4), calls=%async_computation | async-start | bytes 1048576 | tf_op jit(solution)/shard_map/all_to_all | solution.py:281
  14.9 1.3 %collective-permute-start = (bf16[2048,128]{1,0:T(8,128)(2,1)}, bf16[2048,128]{1,0:T(8,128)(2,1)S(1)}, u32[]{:S(2)}, u32[]{:S(2)}) collective-permute-start(bf16[2048,128]{1,0:T(8,128)(2,1)} %bitcast.31), channel_id=1, source_target_pairs={{0,64},{64,128},{128,192},{192,0},{1,65},{65,129},{129,193},{193,1... | collective-permute-start | bytes 1572872 | tf_op jit(solution)/shard_map/ppermute | solution.py:266
  16.2 1.5 %collective-permute-start.2 = (bf16[2048,128]{1,0:T(8,128)(2,1)}, bf16[2048,128]{1,0:T(8,128)(2,1)S(1)}, u32[]{:S(2)}, u32[]{:S(2)}) collective-permute-start(bf16[2048,128]{1,0:T(8,128)(2,1)} %bitcast.34), channel_id=1, source_target_pairs={{0,192},{64,0},{128,64},{192,128},{1,193},{65,1},{129,65},{193,129... | collective-permute-start | bytes 1572872 | tf_op jit(solution)/shard_map/ppermute | solution.py:266
  17.6 1.3 %collective-permute-start.4 = (bf16[2048,128]{1,0:T(8,128)(2,1)}, bf16[2048,128]{1,0:T(8,128)(2,1)S(1)}, u32[]{:S(2)}, u32[]{:S(2)}) collective-permute-start(bf16[2048,128]{1,0:T(8,128)(2,1)} %bitcast.32), channel_id=1, source_target_pairs={{0,192},{64,0},{128,64},{192,128},{1,193},{65,1},{129,65},{193,129... | collective-permute-start | bytes 1572872 | tf_op jit(solution)/shard_map/ppermute | solution.py:266
  18.9 0.2 collective-permute-start.5
  19.1 10.3 %collective-permute-done.refs_1_ = bf16[2048,128]{1,0:T(8,128)(2,1)S(1)} collective-permute-done((bf16[2048,128]{1,0:T(8,128)(2,1)}, bf16[2048,128]{1,0:T(8,128)(2,1)S(1)}, u32[]{:S(2)}, u32[]{:S(2)}) %collective-permute-start) | collective-permute-done | bytes 524320 | tf_op jit(solution)/shard_map/ppermute | solution.py:266
  29.4 0.0 collective-permute-start.1
  29.4 0.0 collective-permute-done.2.refs_4_
  29.4 2.7 %collective-permute-start.3 = (bf16[2048,128]{1,0:T(8,128)(2,1)S(1)}, bf16[2048,128]{1,0:T(8,128)(2,1)S(1)}, u32[]{:S(2)}, u32[]{:S(2)}) collective-permute-start(bf16[2048,128]{1,0:T(8,128)(2,1)S(1)} %collective-permute-done.2.refs_4_), channel_id=1, source_target_pairs={{0,192},{64,0},{128,64},{192,128},{1,193},{65,1},{129,65},{193,129... | collective-permute-start | bytes 1572872 | tf_op jit(solution)/shard_map/ppermute | solution.py:266
  32.1 0.5 all-to-all-done
  32.6 0.0 copy-start.6
  32.6 1.0 %copy-done.6 = bf16[2048,1,128]{2,0,1:T(8,128)(2,1)S(1)} copy-done((bf16[2048,1,128]{2,0,1:T(8,128)(2,1)S(1)}, bf16[2048,1,128]{2,0,1:T(8,128)(2,1)}, u32[]{:S(2)}) %copy-start.6) | copy-done | bytes 524312
  33.6 0.0 copy-start.7
  33.6 1.0 %copy-done.7 = bf16[2048,1,128]{2,0,1:T(8,128)(2,1)S(1)} copy-done((bf16[2048,1,128]{2,0,1:T(8,128)(2,1)S(1)}, bf16[2048,1,128]{2,0,1:T(8,128)(2,1)}, u32[]{:S(2)}) %copy-start.7) | copy-done | bytes 524312
  34.7 5.8 %prompt.3 = (f32[2048,128]{1,0:T(8,128)S(1)}, f32[2048,128]{1,0:T(8,128)S(1)}) custom-call(bf16[2048,128]{1,0:T(8,128)(2,1)S(1)} %bitcast.24, bf16[2048,128]{1,0:T(8,128)(2,1)S(1)} %bitcast.33, bf16[2048,128]{1,0:T(8,128)(2,1)S(1)} %bitcast.36), custom_call_target="tpu_custom_call" | custom-call | flops 2147483648 | bytes 2621440 | tf_op jit(solution)/shard_map/prompt/pallas_call | solution.py:125
  40.5 0.0 collective-permute-done.4.refs_2_
  40.5 0.3 collective-permute-done.5.refs_3_
  40.8 12.6 %prompt.4 = (f32[2048,128]{1,0:T(8,128)S(1)}, f32[2048,128]{1,0:T(8,128)S(1)}) custom-call(bf16[2048,128]{1,0:T(8,128)(2,1)S(1)} %bitcast.25, bf16[2048,128]{1,0:T(8,128)(2,1)S(1)} %collective-permute-done.refs_1_, bf16[2048,128]{1,0:T(8,128)(2,1)S(1)} %collective-permute-done.4.refs_2_, bf16[2048,128]{1,0:T(8,128)(2,1)} %collective-permute-done.5.refs_3_, ...), custom_call_target="tpu_custom_call" | custom-call | flops 4294967296 | bytes 3670016 | tf_op jit(solution)/shard_map/prompt/pallas_call | solution.py:125
  53.3 0.0 collective-permute-done.1.refs_1_
  53.4 0.0 collective-permute-done.3.refs_2_
  53.4 0.0 copy-start.2
  53.4 0.0 copy-start.3
  53.4 0.0 copy-start.4
  53.4 0.0 copy-start.5
  53.4 8.8 %prompt.5 = bf16[64,40,128]{2,1,0:T(8,128)(2,1)} custom-call(bf16[2048,128]{1,0:T(8,128)(2,1)S(1)} %bitcast.26, bf16[2048,128]{1,0:T(8,128)(2,1)S(1)} %collective-permute-done.1.refs_1_, bf16[2048,128]{1,0:T(8,128)(2,1)S(1)} %collective-permute-done.3.refs_2_, f32[2048,128]{1,0:T(8,128)S(1)} %get-tuple-element.13.refs_3_, ...), custom_call_target="tpu_custom_call" | custom-call | flops 2147483648 | bytes 2621440 | tf_op jit(solution)/shard_map/prompt/pallas_call | solution.py:125
  62.2 12.2 %all-to-all-start.1 = ((bf16[64,40,128]{2,1,0:T(8,128)(2,1)}), bf16[64,40,128]{2,1,0:T(8,128)(2,1)S(1)}, u32[]{:S(2)}, u32[]{:S(2)}) async-start(bf16[64,40,128]{2,1,0:T(8,128)(2,1)} %prompt.5), calls=%async_computation.1 | async-start | bytes 1310720 | tf_op jit(solution)/shard_map/all_to_all | solution.py:301
  74.4 0.0 copy-done.2
  74.4 0.0 copy-done.3
  74.4 0.0 copy-done.4
  74.4 0.0 copy-done.5
  74.5 0.0 copy-start
  74.5 2.2 %copy-done = bf16[2,1024,8,128]{3,2,1,0:T(8,128)(2,1)S(1)} copy-done((bf16[2,1024,8,128]{3,2,1,0:T(8,128)(2,1)S(1)}, bf16[2,1024,8,128]{3,2,1,0:T(8,128)(2,1)}, u32[]{:S(2)}) %copy-start) | copy-done | bytes 4194328
  76.6 0.0 copy-start.1
  76.6 2.2 %copy-done.1 = bf16[2,1024,8,128]{3,2,1,0:T(8,128)(2,1)S(1)} copy-done((bf16[2,1024,8,128]{3,2,1,0:T(8,128)(2,1)S(1)}, bf16[2,1024,8,128]{3,2,1,0:T(8,128)(2,1)}, u32[]{:S(2)}) %copy-start.1) | copy-done | bytes 4194328
  78.8 5.4 %suffix.1 = (f32[2,128,128]{2,1,0:T(8,128)S(1)}, f32[2,128,128]{2,1,0:T(8,128)S(1)}) custom-call(bf16[2,128,128]{2,1,0:T(8,128)(2,1)S(1)} %bitcast.28, bf16[2,8192,128]{2,1,0:T(8,128)(2,1)S(1)} %bitcast.22, bf16[2,8192,128]{2,1,0:T(8,128)(2,1)S(1)} %bitcast.23, bf16[2,16,128]{2,1,0:T(8,128)(2,1)S(1)} %bitcast.29, bf16[2,16,128]{2,1,0:T(8,128)(2,1)S(1)} %bitcast.30, ...), custom_call_target="tpu_custom_call" | custom-call | flops 1073741824 | bytes 8388608 | tf_op jit(solution)/shard_map/suffix/pallas_call | solution.py:189
  84.2 10.5 %all-to-all-done.1.got_ref = bf16[64,40,128]{2,1,0:T(8,128)(2,1)S(1)} async-done(((bf16[64,40,128]{2,1,0:T(8,128)(2,1)}), bf16[64,40,128]{2,1,0:T(8,128)(2,1)S(1)}, u32[]{:S(2)}, u32[]{:S(2)}) %all-to-all-start.1) | async-done | bytes 655392 | tf_op jit(solution)/shard_map/all_to_all | solution.py:301
  94.8 1.6 %merge.1 = bf16[2,128,128]{2,1,0:T(8,128)(2,1)} custom-call(bf16[64,40,128]{2,1,0:T(8,128)(2,1)S(1)} %all-to-all-done.1.got_ref, f32[2,128,128]{2,1,0:T(8,128)S(1)} %get-tuple-element.15.own_ref, f32[2,128,128]{2,1,0:T(8,128)S(1)} %get-tuple-element.16.own_level_ref), custom_call_target="tpu_custom_call" | custom-call | tf_op jit(solution)/shard_map/merge/pallas_call | solution.py:249
Async XLA Ops:
  1.7 30.9 %all-to-all-start = ((bf16[64,32,128]{2,1,0:T(8,128)(2,1)}), bf16[64,32,128]{2,1,0:T(8,128)(2,1)S(1)}, u32[]{:S(2)}, u32[]{:S(2)}) async-start(bf16[64,32,128]{2,1,0:T(8,128)(2,1)} %bitcast.4), calls=%async_computation | async-start | bytes 1048576 | tf_op jit(solution)/shard_map/all_to_all | solution.py:281
  14.9 14.5 %collective-permute-start = (bf16[2048,128]{1,0:T(8,128)(2,1)}, bf16[2048,128]{1,0:T(8,128)(2,1)S(1)}, u32[]{:S(2)}, u32[]{:S(2)}) collective-permute-start(bf16[2048,128]{1,0:T(8,128)(2,1)} %bitcast.31), channel_id=1, source_target_pairs={{0,64},{64,128},{128,192},{192,0},{1,65},{65,129},{129,193},{193,1... | collective-permute-start | bytes 1572872 | tf_op jit(solution)/shard_map/ppermute | solution.py:266
  16.2 13.3 %collective-permute-start.2 = (bf16[2048,128]{1,0:T(8,128)(2,1)}, bf16[2048,128]{1,0:T(8,128)(2,1)S(1)}, u32[]{:S(2)}, u32[]{:S(2)}) collective-permute-start(bf16[2048,128]{1,0:T(8,128)(2,1)} %bitcast.34), channel_id=1, source_target_pairs={{0,192},{64,0},{128,64},{192,128},{1,193},{65,1},{129,65},{193,129... | collective-permute-start | bytes 1572872 | tf_op jit(solution)/shard_map/ppermute | solution.py:266
  17.6 22.9 %collective-permute-start.4 = (bf16[2048,128]{1,0:T(8,128)(2,1)}, bf16[2048,128]{1,0:T(8,128)(2,1)S(1)}, u32[]{:S(2)}, u32[]{:S(2)}) collective-permute-start(bf16[2048,128]{1,0:T(8,128)(2,1)} %bitcast.32), channel_id=1, source_target_pairs={{0,192},{64,0},{128,64},{192,128},{1,193},{65,1},{129,65},{193,129... | collective-permute-start | bytes 1572872 | tf_op jit(solution)/shard_map/ppermute | solution.py:266
  18.9 21.9 %collective-permute-start.5 = (bf16[2048,128]{1,0:T(8,128)(2,1)}, bf16[2048,128]{1,0:T(8,128)(2,1)}, u32[]{:S(2)}, u32[]{:S(2)}) collective-permute-start(bf16[2048,128]{1,0:T(8,128)(2,1)} %bitcast.35), channel_id=1, source_target_pairs={{0,64},{64,128},{128,192},{192,0},{1,65},{65,129},{129,193},{193,1... | collective-permute-start | bytes 1572872 | tf_op jit(solution)/shard_map/ppermute | solution.py:266
  29.4 23.9 %collective-permute-start.1 = (bf16[2048,128]{1,0:T(8,128)(2,1)S(1)}, bf16[2048,128]{1,0:T(8,128)(2,1)S(1)}, u32[]{:S(2)}, u32[]{:S(2)}) collective-permute-start(bf16[2048,128]{1,0:T(8,128)(2,1)S(1)} %collective-permute-done.refs_1_), channel_id=1, source_target_pairs={{0,64},{64,128},{128,192},{192,0},{1,65},{65,129},{129,193},{193,1... | collective-permute-start | bytes 1572872 | tf_op jit(solution)/shard_map/ppermute | solution.py:266
  29.4 23.9 %collective-permute-start.3 = (bf16[2048,128]{1,0:T(8,128)(2,1)S(1)}, bf16[2048,128]{1,0:T(8,128)(2,1)S(1)}, u32[]{:S(2)}, u32[]{:S(2)}) collective-permute-start(bf16[2048,128]{1,0:T(8,128)(2,1)S(1)} %collective-permute-done.2.refs_4_), channel_id=1, source_target_pairs={{0,192},{64,0},{128,64},{192,128},{1,193},{65,1},{129,65},{193,129... | collective-permute-start | bytes 1572872 | tf_op jit(solution)/shard_map/ppermute | solution.py:266
  32.6 1.0 %copy-start.6 = (bf16[2048,1,128]{2,0,1:T(8,128)(2,1)S(1)}, bf16[2048,1,128]{2,0,1:T(8,128)(2,1)}, u32[]{:S(2)}) copy-start(bf16[2048,1,128]{2,0,1:T(8,128)(2,1)} %param.9) | copy-start | bytes 1572868
  33.6 1.0 %copy-start.7 = (bf16[2048,1,128]{2,0,1:T(8,128)(2,1)S(1)}, bf16[2048,1,128]{2,0,1:T(8,128)(2,1)}, u32[]{:S(2)}) copy-start(bf16[2048,1,128]{2,0,1:T(8,128)(2,1)} %param.10) | copy-start | bytes 1572868
  53.4 21.0 %copy-start.2 = (bf16[2,2,8192]{2,1,0:T(2,128)(2,1)S(1)}, bf16[2,2,8192]{2,1,0:T(2,128)(2,1)}, u32[]{:S(2)}) copy-start(bf16[2,2,8192]{2,1,0:T(2,128)(2,1)} %param.8) | copy-start | bytes 196612
  53.4 21.0 %copy-start.3 = (bf16[2,2,8,128]{3,2,1,0:T(8,128)(2,1)S(1)}, bf16[2,2,8,128]{3,2,1,0:T(8,128)(2,1)}, u32[]{:S(2)}) copy-start(bf16[2,2,8,128]{3,2,1,0:T(8,128)(2,1)} %param.13) | copy-start | bytes 24580
  53.4 21.0 %copy-start.4 = (bf16[2,2,8,128]{3,2,1,0:T(8,128)(2,1)S(1)}, bf16[2,2,8,128]{3,2,1,0:T(8,128)(2,1)}, u32[]{:S(2)}) copy-start(bf16[2,2,8,128]{3,2,1,0:T(8,128)(2,1)} %param.14) | copy-start | bytes 24580
  53.4 21.0 %copy-start.5 = (s32[2]{0:T(128)S(1)}, s32[2]{0:T(128)}, u32[]{:S(2)}) copy-start(s32[2]{0:T(128)} %len_ref.1) | copy-start | bytes 28
  62.2 32.6 %all-to-all-start.1 = ((bf16[64,40,128]{2,1,0:T(8,128)(2,1)}), bf16[64,40,128]{2,1,0:T(8,128)(2,1)S(1)}, u32[]{:S(2)}, u32[]{:S(2)}) async-start(bf16[64,40,128]{2,1,0:T(8,128)(2,1)} %prompt.5), calls=%async_computation.1 | async-start | bytes 1310720 | tf_op jit(solution)/shard_map/all_to_all | solution.py:301
  74.5 2.2 %copy-start = (bf16[2,1024,8,128]{3,2,1,0:T(8,128)(2,1)S(1)}, bf16[2,1024,8,128]{3,2,1,0:T(8,128)(2,1)}, u32[]{:S(2)}) copy-start(bf16[2,1024,8,128]{3,2,1,0:T(8,128)(2,1)} %param.11) | copy-start | bytes 12582916
  76.6 2.2 %copy-start.1 = (bf16[2,1024,8,128]{3,2,1,0:T(8,128)(2,1)S(1)}, bf16[2,1024,8,128]{3,2,1,0:T(8,128)(2,1)}, u32[]{:S(2)}) copy-start(bf16[2,1024,8,128]{3,2,1,0:T(8,128)(2,1)} %param.12) | copy-start | bytes 12582916

commit v3 on v2

--- a/solution.py
+++ b/solution.py
@@ -130,9 +130,9 @@
         out_shape=out_shape,
         compiler_params=pltpu.CompilerParams(vmem_limit_bytes=VMEM_BYTES),
         cost_estimate=pl.CostEstimate(
-            flops=4 * work * head_dim,
+            flops=work,
             bytes_accessed=4 * blocks * positions * head_dim + 6 * rows * head_dim,
-            transcendentals=work,
+            transcendentals=0,
         ),
         name="prompt",
     )(q, *keys, *values, *carry)
@@ -267,6 +267,9 @@
 
     keys_left, values_left = shift(keys, 1), shift(values, 1)
     keys_right, values_right = shift(keys, -1), shift(values, -1)
+    keys_left, values_left, keys_right, values_right = lax.optimization_barrier(
+        (keys_left, values_left, keys_right, values_right)
+    )
     keys_far, values_far = shift(keys_left, 1), shift(values_right, -1)
 
     per_dest = samples * steps * per_group
@@ -295,8 +298,7 @@
         sub = 128 if final else 256
         return prompt_call(rows, some_keys, some_values, carry, final, 1024, sub, 2048, scale, per_dest)
 
-    carry = prompt([keys], [values], None, False)
-    carry = prompt([keys_left, keys_right], [values_left, values_right], carry, False)
+    carry = prompt([keys, keys_left, keys_right], [values, values_left, values_right], None, False)
     coded = prompt([keys_far], [values_far], carry, True)
     got = lax.all_to_all(coded, ("z", "dec"), 0, 0, tiled=True)
     out = merge_call(got, own, own_level, z_size, groups)

time: 96.9 us -> 94.3 us (0.973)
  starting transfers between devices: 32.3 us -> 27.4 us
  waiting for transfers between devices: 21.6 us -> 25.6 us
  Pallas kernels: 34.2 us -> 32.6 us
    all_to_all x1, waiting for transfers between devices: 0.49 us -> 8.32 us  [local(): lax.all_to_all(spread, ('z', 'dec'), 0, 0, tiled=True).reshape(-1, head_dim)]
    all_to_all x1, starting transfers between devices: 12.2 us -> 6.28 us  [local(): got = lax.all_to_all(coded, ('z', 'dec'), 0, 0, tiled=True)]
    ppermute x6, waiting for transfers between devices: 10.6 us -> 6.72 us  [shift(): lax.ppermute(array, 'x', [(i, (i + amount) % x_size) for i in range(x_siz...]
    pallas_call x3 -> x2, Pallas kernels: 27.1 us -> 25.5 us  [prompt_call(): pl.pallas_call(functools.partial(prompt_kernel, blocks, scale, bool(carry...]
  transfers between devices with their start and end apart: 8 -> 8, of which waited for: 4 -> 4; matrix products, arithmetic and copies ran while one was open for 0% -> 2% of each run, Pallas kernels for 25% -> 23%
where the time goes in v3:
time: 94.3 us; the launch traced here: 93.8 us
  Pallas kernels  32.6 us (35%)
  starting transfers between devices  27.4 us (29%)
  waiting for transfers between devices  25.6 us (27%)
  local copies, waits for them, and re-layouts  8.2 us (9%)
    pallas_call x2, Pallas kernels, prompt_call(): pl.pallas_call(functools.partial(prompt_kernel, blocks, scale, bool(carry...  25.5 us
    all_to_all x1, starting transfers between devices, local(): lax.all_to_all(spread, ('z', 'dec'), 0, 0, tiled=True).reshape(-1, head_dim)  13.6 us
    all_to_all x1, waiting for transfers between devices, local(): got = lax.all_to_all(coded, ('z', 'dec'), 0, 0, tiled=True)  10.5 us
    all_to_all x1, waiting for transfers between devices, local(): lax.all_to_all(spread, ('z', 'dec'), 0, 0, tiled=True).reshape(-1, head_dim)  8.32 us
    ppermute x6, starting transfers between devices, shift(): lax.ppermute(array, 'x', [(i, (i + amount) % x_size) for i in range(x_siz...  7.48 us
    ppermute x6, waiting for transfers between devices, shift(): lax.ppermute(array, 'x', [(i, (i + amount) % x_size) for i in range(x_siz...  6.72 us
    unnamed x16, local copies, waits for them, and re-layouts  6.47 us
    all_to_all x1, starting transfers between devices, local(): got = lax.all_to_all(coded, ('z', 'dec'), 0, 0, tiled=True)  6.28 us
  transfers between devices with their start and end apart: 8, of which 4 were waited for; matrix products, arithmetic and copies ran while one was open for 2% of the time, Pallas kernels for 23%

profile of v3, /device:TPU:1, one launch (start us, length us, event | category | flops | bytes accessed | tf_op | source)
XLA Modules:
  0.0 93.8 jit_solution(983092246960806017)
XLA Ops:
  0.0 2.0 %collective-permute-start = (bf16[2048,128]{1,0:T(8,128)(2,1)}, bf16[2048,128]{1,0:T(8,128)(2,1)S(1)}, u32[]{:S(2)}, u32[]{:S(2)}) collective-permute-start(bf16[2048,128]{1,0:T(8,128)(2,1)} %bitcast.26), channel_id=1, source_target_pairs={{0,64},{64,128},{128,192},{192,0},{1,65},{65,129},{129,193},{193,1... | collective-permute-start | bytes 1572872 | tf_op jit(solution)/shard_map/ppermute | solution.py:266
  2.0 1.2 %collective-permute-start.1 = (bf16[2048,128]{1,0:T(8,128)(2,1)}, bf16[2048,128]{1,0:T(8,128)(2,1)S(1)}, u32[]{:S(2)}, u32[]{:S(2)}) collective-permute-start(bf16[2048,128]{1,0:T(8,128)(2,1)} %bitcast.29), channel_id=1, source_target_pairs={{0,64},{64,128},{128,192},{192,0},{1,65},{65,129},{129,193},{193,1... | collective-permute-start | bytes 1572872 | tf_op jit(solution)/shard_map/ppermute | solution.py:266
  3.3 1.5 %collective-permute-start.2 = (bf16[2048,128]{1,0:T(8,128)(2,1)}, bf16[2048,128]{1,0:T(8,128)(2,1)S(1)}, u32[]{:S(2)}, u32[]{:S(2)}) collective-permute-start(bf16[2048,128]{1,0:T(8,128)(2,1)} %bitcast.27), channel_id=1, source_target_pairs={{0,192},{64,0},{128,64},{192,128},{1,193},{65,1},{129,65},{193,129... | collective-permute-start | bytes 1572872 | tf_op jit(solution)/shard_map/ppermute | solution.py:266
  4.7 0.1 collective-permute-start.3
  4.8 0.8 copy.10
  5.7 0.9 broadcast_in_dim.2
  6.5 13.6 %all-to-all-start = ((bf16[64,32,128]{2,1,0:T(8,128)(2,1)}), bf16[64,32,128]{2,1,0:T(8,128)(2,1)S(1)}, u32[]{:S(2)}, u32[]{:S(2)}) async-start(bf16[64,32,128]{2,1,0:T(8,128)(2,1)} %bitcast.4), calls=%async_computation | async-start | bytes 1048576 | tf_op jit(solution)/shard_map/all_to_all | solution.py:284
  20.2 0.0 collective-permute-done.refs_2_
  20.2 3.9 %collective-permute-done.1.refs_5_ = bf16[2048,128]{1,0:T(8,128)(2,1)S(1)} collective-permute-done((bf16[2048,128]{1,0:T(8,128)(2,1)}, bf16[2048,128]{1,0:T(8,128)(2,1)S(1)}, u32[]{:S(2)}, u32[]{:S(2)}) %collective-permute-start.1) | collective-permute-done | bytes 524320 | tf_op jit(solution)/shard_map/ppermute | solution.py:266
  24.1 0.0 collective-permute-done.2.refs_3_
  24.1 2.8 %collective-permute-done.3.refs_6_ = bf16[2048,128]{1,0:T(8,128)(2,1)S(1)} collective-permute-done((bf16[2048,128]{1,0:T(8,128)(2,1)}, bf16[2048,128]{1,0:T(8,128)(2,1)S(1)}, u32[]{:S(2)}, u32[]{:S(2)}) %collective-permute-start.3) | collective-permute-done | bytes 524320 | tf_op jit(solution)/shard_map/ppermute | solution.py:266
  26.9 0.7 collective-permute-start.4
  27.6 1.9 %collective-permute-start.5 = (bf16[2048,128]{1,0:T(8,128)(2,1)S(1)}, bf16[2048,128]{1,0:T(8,128)(2,1)}, u32[]{:S(2)}, u32[]{:S(2)}) collective-permute-start(bf16[2048,128]{1,0:T(8,128)(2,1)S(1)} %collective-permute-done.3.refs_6_), channel_id=1, source_target_pairs={{0,192},{64,0},{128,64},{192,128},{1,193},{65,1},{129,65},{193,129... | collective-permute-start | bytes 1572872 | tf_op jit(solution)/shard_map/ppermute | solution.py:266
  29.6 8.3 %all-to-all-done = bf16[64,32,128]{2,1,0:T(8,128)(2,1)S(1)} async-done(((bf16[64,32,128]{2,1,0:T(8,128)(2,1)}), bf16[64,32,128]{2,1,0:T(8,128)(2,1)S(1)}, u32[]{:S(2)}, u32[]{:S(2)}) %all-to-all-start) | async-done | bytes 524320 | tf_op jit(solution)/shard_map/all_to_all | solution.py:284
  37.9 0.0 copy-start.2
  37.9 1.0 %copy-done.2 = bf16[2048,1,128]{2,0,1:T(8,128)(2,1)S(1)} copy-done((bf16[2048,1,128]{2,0,1:T(8,128)(2,1)S(1)}, bf16[2048,1,128]{2,0,1:T(8,128)(2,1)}, u32[]{:S(2)}) %copy-start.2) | copy-done | bytes 524312
  38.9 0.0 copy-start.3
  38.9 1.0 %copy-done.3 = bf16[2048,1,128]{2,0,1:T(8,128)(2,1)S(1)} copy-done((bf16[2048,1,128]{2,0,1:T(8,128)(2,1)S(1)}, bf16[2048,1,128]{2,0,1:T(8,128)(2,1)}, u32[]{:S(2)}) %copy-start.3) | copy-done | bytes 524312
  40.0 0.0 copy-start.4
  40.0 0.0 copy-start.5
  40.0 0.0 copy-start.6
  40.0 0.0 copy-start.7
  40.0 15.9 %prompt.2 = (f32[2048,128]{1,0:T(8,128)S(1)}, f32[2048,128]{1,0:T(8,128)S(1)}) custom-call(bf16[2048,128]{1,0:T(8,128)(2,1)S(1)} %bitcast.22, bf16[2048,128]{1,0:T(8,128)(2,1)S(1)} %bitcast.28, bf16[2048,128]{1,0:T(8,128)(2,1)S(1)} %collective-permute-done.refs_2_, bf16[2048,128]{1,0:T(8,128)(2,1)S(1)} %collective-permute-done.2.refs_3_, ...), custom_call_target="tpu_custom_call" | custom-call | flops 12582912 | bytes 4718592 | tf_op jit(solution)/shard_map/prompt/pallas_call | solution.py:125
  55.8 0.0 collective-permute-done.4.refs_1_
  55.9 0.0 collective-permute-done.5.refs_2_
  55.9 9.6 %prompt.3 = bf16[64,40,128]{2,1,0:T(8,128)(2,1)} custom-call(bf16[2048,128]{1,0:T(8,128)(2,1)S(1)} %bitcast.23, bf16[2048,128]{1,0:T(8,128)(2,1)S(1)} %collective-permute-done.4.refs_1_, bf16[2048,128]{1,0:T(8,128)(2,1)} %collective-permute-done.5.refs_2_, f32[2048,128]{1,0:T(8,128)S(1)} %get-tuple-element.17.refs_3_, f32[2048,128]{1,0:T(8,128)S(1)} %get-tuple-element.18.refs_4_), custom_call_target="tpu_custom_call" | custom-call | flops 4194304 | bytes 2621440 | tf_op jit(solution)/shard_map/prompt/pallas_call | solution.py:125
  65.5 6.3 %all-to-all-start.1 = ((bf16[64,40,128]{2,1,0:T(8,128)(2,1)}), bf16[64,40,128]{2,1,0:T(8,128)(2,1)S(1)}, u32[]{:S(2)}, u32[]{:S(2)}) async-start(bf16[64,40,128]{2,1,0:T(8,128)(2,1)} %prompt.3), calls=%async_computation.1 | async-start | bytes 1310720 | tf_op jit(solution)/shard_map/all_to_all | solution.py:303
  71.8 0.0 copy-done.4
  71.8 0.0 copy-done.5
  71.8 0.0 copy-done.6
  71.8 0.0 copy-done.7
  71.8 0.0 copy-start
  71.8 2.2 %copy-done = bf16[2,1024,8,128]{3,2,1,0:T(8,128)(2,1)S(1)} copy-done((bf16[2,1024,8,128]{3,2,1,0:T(8,128)(2,1)S(1)}, bf16[2,1024,8,128]{3,2,1,0:T(8,128)(2,1)}, u32[]{:S(2)}) %copy-start) | copy-done | bytes 4194328
  74.0 0.0 copy-start.1
  74.0 2.2 %copy-done.1 = bf16[2,1024,8,128]{3,2,1,0:T(8,128)(2,1)S(1)} copy-done((bf16[2,1024,8,128]{3,2,1,0:T(8,128)(2,1)S(1)}, bf16[2,1024,8,128]{3,2,1,0:T(8,128)(2,1)}, u32[]{:S(2)}) %copy-start.1) | copy-done | bytes 4194328
  76.2 5.4 %suffix.1 = (f32[2,128,128]{2,1,0:T(8,128)S(1)}, f32[2,128,128]{2,1,0:T(8,128)S(1)}) custom-call(bf16[2,128,128]{2,1,0:T(8,128)(2,1)S(1)} %bitcast.33, bf16[2,8192,128]{2,1,0:T(8,128)(2,1)S(1)} %bitcast.24, bf16[2,8192,128]{2,1,0:T(8,128)(2,1)S(1)} %bitcast.25, bf16[2,16,128]{2,1,0:T(8,128)(2,1)S(1)} %bitcast.34, bf16[2,16,128]{2,1,0:T(8,128)(2,1)S(1)} %bitcast.35, ...), custom_call_target="tpu_custom_call" | custom-call | flops 1073741824 | bytes 8388608 | tf_op jit(solution)/shard_map/suffix/pallas_call | solution.py:189
  81.6 10.5 %all-to-all-done.1.got_ref = bf16[64,40,128]{2,1,0:T(8,128)(2,1)S(1)} async-done(((bf16[64,40,128]{2,1,0:T(8,128)(2,1)}), bf16[64,40,128]{2,1,0:T(8,128)(2,1)S(1)}, u32[]{:S(2)}, u32[]{:S(2)}) %all-to-all-start.1) | async-done | bytes 655392 | tf_op jit(solution)/shard_map/all_to_all | solution.py:303
  92.2 1.6 %merge.1 = bf16[2,128,128]{2,1,0:T(8,128)(2,1)} custom-call(bf16[64,40,128]{2,1,0:T(8,128)(2,1)S(1)} %all-to-all-done.1.got_ref, f32[2,128,128]{2,1,0:T(8,128)S(1)} %get-tuple-element.19.own_ref, f32[2,128,128]{2,1,0:T(8,128)S(1)} %get-tuple-element.20.own_level_ref), custom_call_target="tpu_custom_call" | custom-call | tf_op jit(solution)/shard_map/merge/pallas_call | solution.py:249
Async XLA Ops:
  0.0 20.2 %collective-permute-start = (bf16[2048,128]{1,0:T(8,128)(2,1)}, bf16[2048,128]{1,0:T(8,128)(2,1)S(1)}, u32[]{:S(2)}, u32[]{:S(2)}) collective-permute-start(bf16[2048,128]{1,0:T(8,128)(2,1)} %bitcast.26), channel_id=1, source_target_pairs={{0,64},{64,128},{128,192},{192,0},{1,65},{65,129},{129,193},{193,1... | collective-permute-start | bytes 1572872 | tf_op jit(solution)/shard_map/ppermute | solution.py:266
  2.0 22.1 %collective-permute-start.1 = (bf16[2048,128]{1,0:T(8,128)(2,1)}, bf16[2048,128]{1,0:T(8,128)(2,1)S(1)}, u32[]{:S(2)}, u32[]{:S(2)}) collective-permute-start(bf16[2048,128]{1,0:T(8,128)(2,1)} %bitcast.29), channel_id=1, source_target_pairs={{0,64},{64,128},{128,192},{192,0},{1,65},{65,129},{129,193},{193,1... | collective-permute-start | bytes 1572872 | tf_op jit(solution)/shard_map/ppermute | solution.py:266
  3.3 20.9 %collective-permute-start.2 = (bf16[2048,128]{1,0:T(8,128)(2,1)}, bf16[2048,128]{1,0:T(8,128)(2,1)S(1)}, u32[]{:S(2)}, u32[]{:S(2)}) collective-permute-start(bf16[2048,128]{1,0:T(8,128)(2,1)} %bitcast.27), channel_id=1, source_target_pairs={{0,192},{64,0},{128,64},{192,128},{1,193},{65,1},{129,65},{193,129... | collective-permute-start | bytes 1572872 | tf_op jit(solution)/shard_map/ppermute | solution.py:266
  4.7 22.2 %collective-permute-start.3 = (bf16[2048,128]{1,0:T(8,128)(2,1)}, bf16[2048,128]{1,0:T(8,128)(2,1)S(1)}, u32[]{:S(2)}, u32[]{:S(2)}) collective-permute-start(bf16[2048,128]{1,0:T(8,128)(2,1)} %bitcast.30), channel_id=1, source_target_pairs={{0,192},{64,0},{128,64},{192,128},{1,193},{65,1},{129,65},{193,129... | collective-permute-start | bytes 1572872 | tf_op jit(solution)/shard_map/ppermute | solution.py:266
  6.5 31.3 %all-to-all-start = ((bf16[64,32,128]{2,1,0:T(8,128)(2,1)}), bf16[64,32,128]{2,1,0:T(8,128)(2,1)S(1)}, u32[]{:S(2)}, u32[]{:S(2)}) async-start(bf16[64,32,128]{2,1,0:T(8,128)(2,1)} %bitcast.4), calls=%async_computation | async-start | bytes 1048576 | tf_op jit(solution)/shard_map/all_to_all | solution.py:284
  26.9 29.0 %collective-permute-start.4 = (bf16[2048,128]{1,0:T(8,128)(2,1)S(1)}, bf16[2048,128]{1,0:T(8,128)(2,1)S(1)}, u32[]{:S(2)}, u32[]{:S(2)}) collective-permute-start(bf16[2048,128]{1,0:T(8,128)(2,1)S(1)} %collective-permute-done.refs_2_), channel_id=1, source_target_pairs={{0,64},{64,128},{128,192},{192,0},{1,65},{65,129},{129,193},{193,1... | collective-permute-start | bytes 1572872 | tf_op jit(solution)/shard_map/ppermute | solution.py:266
  27.6 28.2 %collective-permute-start.5 = (bf16[2048,128]{1,0:T(8,128)(2,1)S(1)}, bf16[2048,128]{1,0:T(8,128)(2,1)}, u32[]{:S(2)}, u32[]{:S(2)}) collective-permute-start(bf16[2048,128]{1,0:T(8,128)(2,1)S(1)} %collective-permute-done.3.refs_6_), channel_id=1, source_target_pairs={{0,192},{64,0},{128,64},{192,128},{1,193},{65,1},{129,65},{193,129... | collective-permute-start | bytes 1572872 | tf_op jit(solution)/shard_map/ppermute | solution.py:266
  37.9 1.0 %copy-start.2 = (bf16[2048,1,128]{2,0,1:T(8,128)(2,1)S(1)}, bf16[2048,1,128]{2,0,1:T(8,128)(2,1)}, u32[]{:S(2)}) copy-start(bf16[2048,1,128]{2,0,1:T(8,128)(2,1)} %param.9) | copy-start | bytes 1572868
  38.9 1.0 %copy-start.3 = (bf16[2048,1,128]{2,0,1:T(8,128)(2,1)S(1)}, bf16[2048,1,128]{2,0,1:T(8,128)(2,1)}, u32[]{:S(2)}) copy-start(bf16[2048,1,128]{2,0,1:T(8,128)(2,1)} %param.10) | copy-start | bytes 1572868
  40.0 31.8 %copy-start.4 = (bf16[2,2,8192]{2,1,0:T(2,128)(2,1)S(1)}, bf16[2,2,8192]{2,1,0:T(2,128)(2,1)}, u32[]{:S(2)}) copy-start(bf16[2,2,8192]{2,1,0:T(2,128)(2,1)} %param.8) | copy-start | bytes 196612
  40.0 31.8 %copy-start.5 = (bf16[2,2,8,128]{3,2,1,0:T(8,128)(2,1)S(1)}, bf16[2,2,8,128]{3,2,1,0:T(8,128)(2,1)}, u32[]{:S(2)}) copy-start(bf16[2,2,8,128]{3,2,1,0:T(8,128)(2,1)} %param.13) | copy-start | bytes 24580
  40.0 31.9 %copy-start.6 = (bf16[2,2,8,128]{3,2,1,0:T(8,128)(2,1)S(1)}, bf16[2,2,8,128]{3,2,1,0:T(8,128)(2,1)}, u32[]{:S(2)}) copy-start(bf16[2,2,8,128]{3,2,1,0:T(8,128)(2,1)} %param.14) | copy-start | bytes 24580
  40.0 31.9 %copy-start.7 = (s32[2]{0:T(128)S(1)}, s32[2]{0:T(128)}, u32[]{:S(2)}) copy-start(s32[2]{0:T(128)} %len_ref.1) | copy-start | bytes 28
  65.5 26.6 %all-to-all-start.1 = ((bf16[64,40,128]{2,1,0:T(8,128)(2,1)}), bf16[64,40,128]{2,1,0:T(8,128)(2,1)S(1)}, u32[]{:S(2)}, u32[]{:S(2)}) async-start(bf16[64,40,128]{2,1,0:T(8,128)(2,1)} %prompt.3), calls=%async_computation.1 | async-start | bytes 1310720 | tf_op jit(solution)/shard_map/all_to_all | solution.py:303
  71.8 2.2 %copy-start = (bf16[2,1024,8,128]{3,2,1,0:T(8,128)(2,1)S(1)}, bf16[2,1024,8,128]{3,2,1,0:T(8,128)(2,1)}, u32[]{:S(2)}) copy-start(bf16[2,1024,8,128]{3,2,1,0:T(8,128)(2,1)} %param.11) | copy-start | bytes 12582916
  74.0 2.2 %copy-start.1 = (bf16[2,1024,8,128]{3,2,1,0:T(8,128)(2,1)S(1)}, bf16[2,1024,8,128]{3,2,1,0:T(8,128)(2,1)}, u32[]{:S(2)}) copy-start(bf16[2,1024,8,128]{3,2,1,0:T(8,128)(2,1)} %param.12) | copy-start | bytes 12582916

commit v4 on v3

--- a/solution.py
+++ b/solution.py
@@ -26,16 +26,28 @@
     return hi, mid, x - hi - mid
 
 
-def prompt_kernel(blocks, scale, carried, final, sub, chunk, per_dest, *refs):
+def prompt_kernel(blocks, late, scale, carried, final, sub, chunk, per_dest, *refs):
     q_ref = refs[0]
-    k_refs = refs[1 : 1 + blocks]
-    v_refs = refs[1 + blocks : 1 + 2 * blocks]
+    arrays = list(refs[1 : 1 + 2 * blocks])
     rest = refs[1 + 2 * blocks :]
+    copies = {}
+    if late:
+        landing, arrived = refs[-2:]
+        for n, at in enumerate(late):
+            copies[at] = pltpu.make_async_copy(arrays[at], landing.at[n], arrived.at[n])
+            copies[at].start()
+            arrays[at] = landing.at[n]
+
+    def block(at, offset):
+        if at in copies:
+            copies.pop(at).wait()
+        return arrays[at][offset : offset + chunk]
+
     if carried:
         acc_in, stat_in = rest[:2]
         rest = rest[2:]
     rows, head_dim = q_ref.shape
-    keys = k_refs[0].shape[0]
+    keys = arrays[0].shape[0]
     items = [
         (start, b, offset)
         for start in range(0, rows, sub)
@@ -45,7 +57,7 @@
 
     def score(item):
         start, b, offset = item
-        return dot_nt(q_ref[start : start + sub], k_refs[b][offset : offset + chunk])
+        return dot_nt(q_ref[start : start + sub], block(b, offset))
 
     def finish(start, acc, top, total):
         if final:
@@ -73,7 +85,7 @@
         new_top = part_top if acc is None else jnp.maximum(top, part_top)
         weights = jnp.exp2((scores - new_top) * scale)
         part_total = jnp.sum(weights, axis=1, keepdims=True)
-        part = jnp.dot(weights.astype(BF16), v_refs[b][offset : offset + chunk], preferred_element_type=F32)
+        part = jnp.dot(weights.astype(BF16), block(blocks + b, offset), preferred_element_type=F32)
         if acc is None:
             acc, total = part, part_total
         else:
@@ -107,27 +119,27 @@
         out_ref[first + i, per_dest : per_dest + STAT_ROWS, :] = packed.astype(BF16)
 
 
-def prompt_call(q, keys, values, carry, final, tile, sub, chunk, scale, per_dest):
+def prompt_call(q, keys, values, late, carry, final, sub, chunk, scale, per_dest):
     rows, head_dim = q.shape
     positions = keys[0].shape[0]
     blocks = len(keys)
-    row_spec = pl.BlockSpec((tile, head_dim), lambda i: (i, 0))
-    full = pl.BlockSpec((positions, head_dim), lambda i: (0, 0))
+    whole = pl.BlockSpec(memory_space=pltpu.VMEM)
     if final:
-        dests = rows // per_dest
-        out_specs = pl.BlockSpec((tile // per_dest, per_dest + STAT_ROWS, head_dim), lambda i: (i, 0, 0))
-        out_shape = jax.ShapeDtypeStruct((dests, per_dest + STAT_ROWS, head_dim), BF16)
+        out_shape = jax.ShapeDtypeStruct((rows // per_dest, per_dest + STAT_ROWS, head_dim), BF16)
     else:
-        out_specs = [row_spec, row_spec]
         out_shape = [jax.ShapeDtypeStruct((rows, head_dim), F32)] * 2
+    block_specs = [pl.BlockSpec(memory_space=pl.ANY) if at in late else whole for at in range(2 * blocks)]
     carry = [] if carry is None else list(carry)
     work = rows * positions * blocks
     return pl.pallas_call(
-        functools.partial(prompt_kernel, blocks, scale, bool(carry), final, sub, chunk, per_dest),
-        grid=(rows // tile,),
-        in_specs=[row_spec] + [full] * (2 * blocks) + [row_spec] * len(carry),
-        out_specs=out_specs,
+        functools.partial(prompt_kernel, blocks, late, scale, bool(carry), final, sub, chunk, per_dest),
+        in_specs=[whole] + block_specs + [whole] * len(carry),
+        out_specs=whole if final else [whole, whole],
         out_shape=out_shape,
+        scratch_shapes=[
+            pltpu.VMEM((max(len(late), 1), positions, head_dim), BF16),
+            pltpu.SemaphoreType.DMA((max(len(late), 1),)),
+        ],
         compiler_params=pltpu.CompilerParams(vmem_limit_bytes=VMEM_BYTES),
         cost_estimate=pl.CostEstimate(
             flops=work,
@@ -294,12 +306,11 @@
         groups,
         steps,
     )
-    def prompt(some_keys, some_values, carry, final):
-        sub = 128 if final else 256
-        return prompt_call(rows, some_keys, some_values, carry, final, 1024, sub, 2048, scale, per_dest)
-
-    carry = prompt([keys, keys_left, keys_right], [values, values_left, values_right], None, False)
-    coded = prompt([keys_far], [values_far], carry, True)
+    def prompt(some_keys, some_values, late, carry, final, sub):
+        return prompt_call(rows, some_keys, some_values, late, carry, final, sub, 2048, scale, per_dest)
+
+    carry = prompt([keys_left, keys_right], [values_left, values_right], (), None, False, 256)
+    coded = prompt([keys, keys_far], [values, values_far], (1, 3), carry, True, 128)
     got = lax.all_to_all(coded, ("z", "dec"), 0, 0, tiled=True)
     out = merge_call(got, own, own_level, z_size, groups)
     return (

time: 94.3 us -> 92.1 us (0.977)
  local copies, waits for them, and re-layouts: 8.2 us -> 7.15 us
    unnamed x16, local copies, waits for them, and re-layouts: 6.47 us -> 5.43 us
  transfers between devices with their start and end apart: 8 -> 8, of which waited for: 4 -> 4; matrix products, arithmetic and copies ran while one was open for 2% -> 2% of each run, Pallas kernels for 23% -> 17%
where the time goes in v4:
time: 92.1 us; the launch traced here: 91.7 us
  Pallas kernels  31.7 us (34%)
  starting transfers between devices  27.2 us (30%)
  waiting for transfers between devices  25.6 us (28%)
  local copies, waits for them, and re-layouts  7.15 us (8%)
    pallas_call x2, Pallas kernels, prompt_call(): pl.pallas_call(functools.partial(prompt_kernel, blocks, late, scale, bool...  24.6 us
    all_to_all x1, starting transfers between devices, local(): lax.all_to_all(spread, ('z', 'dec'), 0, 0, tiled=True).reshape(-1, head_dim)  13.6 us
    all_to_all x1, waiting for transfers between devices, local(): got = lax.all_to_all(coded, ('z', 'dec'), 0, 0, tiled=True)  10.5 us
    all_to_all x1, waiting for transfers between devices, local(): lax.all_to_all(spread, ('z', 'dec'), 0, 0, tiled=True).reshape(-1, head_dim)  8.32 us
    ppermute x6, starting transfers between devices, shift(): lax.ppermute(array, 'x', [(i, (i + amount) % x_size) for i in range(x_siz...  7.53 us
    ppermute x6, waiting for transfers between devices, shift(): lax.ppermute(array, 'x', [(i, (i + amount) % x_size) for i in range(x_siz...  6.72 us
    all_to_all x1, starting transfers between devices, local(): got = lax.all_to_all(coded, ('z', 'dec'), 0, 0, tiled=True)  6.09 us
    unnamed x16, local copies, waits for them, and re-layouts  5.43 us
  transfers between devices with their start and end apart: 8, of which 4 were waited for; matrix products, arithmetic and copies ran while one was open for 2% of the time, Pallas kernels for 17%

profile of v4, /device:TPU:1, one launch (start us, length us, event | category | flops | bytes accessed | tf_op | source)
XLA Modules:
  0.0 91.7 jit_solution(5767885255878026417)
XLA Ops:
  0.0 0.0 copy-start.2
  0.0 2.0 %collective-permute-start = (bf16[2048,128]{1,0:T(8,128)(2,1)}, bf16[2048,128]{1,0:T(8,128)(2,1)S(1)}, u32[]{:S(2)}, u32[]{:S(2)}) collective-permute-start(bf16[2048,128]{1,0:T(8,128)(2,1)} %bitcast.26), channel_id=1, source_target_pairs={{0,64},{64,128},{128,192},{192,0},{1,65},{65,129},{129,193},{193,1... | collective-permute-start | bytes 1572872 | tf_op jit(solution)/shard_map/ppermute | solution.py:278
  2.0 1.2 %collective-permute-start.1 = (bf16[2048,128]{1,0:T(8,128)(2,1)}, bf16[2048,128]{1,0:T(8,128)(2,1)S(1)}, u32[]{:S(2)}, u32[]{:S(2)}) collective-permute-start(bf16[2048,128]{1,0:T(8,128)(2,1)} %bitcast.29), channel_id=1, source_target_pairs={{0,64},{64,128},{128,192},{192,0},{1,65},{65,129},{129,193},{193,1... | collective-permute-start | bytes 1572872 | tf_op jit(solution)/shard_map/ppermute | solution.py:278
  3.3 1.5 %collective-permute-start.2 = (bf16[2048,128]{1,0:T(8,128)(2,1)}, bf16[2048,128]{1,0:T(8,128)(2,1)S(1)}, u32[]{:S(2)}, u32[]{:S(2)}) collective-permute-start(bf16[2048,128]{1,0:T(8,128)(2,1)} %bitcast.27), channel_id=1, source_target_pairs={{0,192},{64,0},{128,64},{192,128},{1,193},{65,1},{129,65},{193,129... | collective-permute-start | bytes 1572872 | tf_op jit(solution)/shard_map/ppermute | solution.py:278
  4.7 0.1 collective-permute-start.3
  4.9 0.8 copy.10
  5.7 0.9 broadcast_in_dim.2
  6.6 13.6 %all-to-all-start = ((bf16[64,32,128]{2,1,0:T(8,128)(2,1)}), bf16[64,32,128]{2,1,0:T(8,128)(2,1)S(1)}, u32[]{:S(2)}, u32[]{:S(2)}) async-start(bf16[64,32,128]{2,1,0:T(8,128)(2,1)} %bitcast.36), calls=%async_computation | async-start | bytes 1048576 | tf_op jit(solution)/shard_map/all_to_all | solution.py:296
  20.2 0.0 collective-permute-done.refs_1_
  20.2 4.1 %collective-permute-done.1.refs_3_ = bf16[2048,128]{1,0:T(8,128)(2,1)S(1)} collective-permute-done((bf16[2048,128]{1,0:T(8,128)(2,1)}, bf16[2048,128]{1,0:T(8,128)(2,1)S(1)}, u32[]{:S(2)}, u32[]{:S(2)}) %collective-permute-start.1) | collective-permute-done | bytes 524320 | tf_op jit(solution)/shard_map/ppermute | solution.py:278
  24.2 0.0 collective-permute-done.2.refs_2_
  24.3 2.6 %collective-permute-done.3.refs_4_ = bf16[2048,128]{1,0:T(8,128)(2,1)S(1)} collective-permute-done((bf16[2048,128]{1,0:T(8,128)(2,1)}, bf16[2048,128]{1,0:T(8,128)(2,1)S(1)}, u32[]{:S(2)}, u32[]{:S(2)}) %collective-permute-start.3) | collective-permute-done | bytes 524320 | tf_op jit(solution)/shard_map/ppermute | solution.py:278
  26.9 0.7 collective-permute-start.4
  27.6 1.9 %collective-permute-start.5 = (bf16[2048,128]{1,0:T(8,128)(2,1)S(1)}, bf16[2048,128]{1,0:T(8,128)(2,1)}, u32[]{:S(2)}, u32[]{:S(2)}) collective-permute-start(bf16[2048,128]{1,0:T(8,128)(2,1)S(1)} %collective-permute-done.3.refs_4_), channel_id=1, source_target_pairs={{0,192},{64,0},{128,64},{192,128},{1,193},{65,1},{129,65},{193,129... | collective-permute-start | bytes 1572872 | tf_op jit(solution)/shard_map/ppermute | solution.py:278
  29.6 8.3 %all-to-all-done = bf16[64,32,128]{2,1,0:T(8,128)(2,1)S(1)} async-done(((bf16[64,32,128]{2,1,0:T(8,128)(2,1)}), bf16[64,32,128]{2,1,0:T(8,128)(2,1)S(1)}, u32[]{:S(2)}, u32[]{:S(2)}) %all-to-all-start) | async-done | bytes 524320 | tf_op jit(solution)/shard_map/all_to_all | solution.py:296
  37.9 0.0 copy-start.4
  37.9 0.0 copy-start.5
  37.9 0.0 copy-start.6
  37.9 0.0 copy-start.7
  37.9 10.4 %prompt.2 = (f32[2048,128]{1,0:T(8,128)S(1)}, f32[2048,128]{1,0:T(8,128)S(1)}) custom-call(bf16[2048,128]{1,0:T(8,128)(2,1)S(1)} %bitcast.22, bf16[2048,128]{1,0:T(8,128)(2,1)S(1)} %collective-permute-done.refs_1_, bf16[2048,128]{1,0:T(8,128)(2,1)S(1)} %collective-permute-done.2.refs_2_, bf16[2048,128]{1,0:T(8,128)(2,1)S(1)} %collective-permute-done.1.refs_3_, ...), custom_call_target="tpu_custom_call" | custom-call | flops 8388608 | bytes 3670016 | tf_op jit(solution)/shard_map/prompt/pallas_call | solution.py:134
  48.3 0.0 collective-permute-done.4.refs_2_
  48.3 0.0 collective-permute-done.5.refs_4_
  48.3 0.0 copy-done.2
  48.3 0.0 copy-start.3
  48.3 1.0 %copy-done.3 = bf16[2048,1,128]{2,0,1:T(8,128)(2,1)S(1)} copy-done((bf16[2048,1,128]{2,0,1:T(8,128)(2,1)S(1)}, bf16[2048,1,128]{2,0,1:T(8,128)(2,1)}, u32[]{:S(2)}) %copy-start.3) | copy-done | bytes 524312
  49.4 14.3 %prompt.3 = bf16[64,40,128]{2,1,0:T(8,128)(2,1)} custom-call(bf16[2048,128]{1,0:T(8,128)(2,1)S(1)} %bitcast.23, bf16[2048,128]{1,0:T(8,128)(2,1)S(1)} %bitcast.28, bf16[2048,128]{1,0:T(8,128)(2,1)} %collective-permute-done.4.refs_2_, bf16[2048,128]{1,0:T(8,128)(2,1)S(1)} %bitcast.31, bf16[2048,128]{1,0:T(8,128)(2,1)} %collective-permute-done.5.refs_4_, ...), custom_call_target="tpu_custom_call" | custom-call | flops 8388608 | bytes 3670016 | tf_op jit(solution)/shard_map/prompt/pallas_call | solution.py:134
  63.6 6.1 %all-to-all-start.1 = ((bf16[64,40,128]{2,1,0:T(8,128)(2,1)}), bf16[64,40,128]{2,1,0:T(8,128)(2,1)S(1)}, u32[]{:S(2)}, u32[]{:S(2)}) async-start(bf16[64,40,128]{2,1,0:T(8,128)(2,1)} %prompt.3), calls=%async_computation.1 | async-start | bytes 1310720 | tf_op jit(solution)/shard_map/all_to_all | solution.py:314
  69.7 0.0 copy-done.4
  69.7 0.0 copy-done.5
  69.7 0.0 copy-done.6
  69.8 0.0 copy-done.7
  69.8 0.0 copy-start
  69.8 2.2 %copy-done = bf16[2,1024,8,128]{3,2,1,0:T(8,128)(2,1)S(1)} copy-done((bf16[2,1024,8,128]{3,2,1,0:T(8,128)(2,1)S(1)}, bf16[2,1024,8,128]{3,2,1,0:T(8,128)(2,1)}, u32[]{:S(2)}) %copy-start) | copy-done | bytes 4194328
  72.0 0.0 copy-start.1
  72.0 2.2 %copy-done.1 = bf16[2,1024,8,128]{3,2,1,0:T(8,128)(2,1)S(1)} copy-done((bf16[2,1024,8,128]{3,2,1,0:T(8,128)(2,1)S(1)}, bf16[2,1024,8,128]{3,2,1,0:T(8,128)(2,1)}, u32[]{:S(2)}) %copy-start.1) | copy-done | bytes 4194328
  74.1 5.4 %suffix.1 = (f32[2,128,128]{2,1,0:T(8,128)S(1)}, f32[2,128,128]{2,1,0:T(8,128)S(1)}) custom-call(bf16[2,128,128]{2,1,0:T(8,128)(2,1)S(1)} %bitcast.33, bf16[2,8192,128]{2,1,0:T(8,128)(2,1)S(1)} %bitcast.24, bf16[2,8192,128]{2,1,0:T(8,128)(2,1)S(1)} %bitcast.25, bf16[2,16,128]{2,1,0:T(8,128)(2,1)S(1)} %bitcast.34, bf16[2,16,128]{2,1,0:T(8,128)(2,1)S(1)} %bitcast.35, ...), custom_call_target="tpu_custom_call" | custom-call | flops 1073741824 | bytes 8388608 | tf_op jit(solution)/shard_map/suffix/pallas_call | solution.py:201
  79.5 10.5 %all-to-all-done.1.got_ref = bf16[64,40,128]{2,1,0:T(8,128)(2,1)S(1)} async-done(((bf16[64,40,128]{2,1,0:T(8,128)(2,1)}), bf16[64,40,128]{2,1,0:T(8,128)(2,1)S(1)}, u32[]{:S(2)}, u32[]{:S(2)}) %all-to-all-start.1) | async-done | bytes 655392 | tf_op jit(solution)/shard_map/all_to_all | solution.py:314
  90.1 1.6 %merge.1 = bf16[2,128,128]{2,1,0:T(8,128)(2,1)} custom-call(bf16[64,40,128]{2,1,0:T(8,128)(2,1)S(1)} %all-to-all-done.1.got_ref, f32[2,128,128]{2,1,0:T(8,128)S(1)} %get-tuple-element.19.own_ref, f32[2,128,128]{2,1,0:T(8,128)S(1)} %get-tuple-element.20.own_level_ref), custom_call_target="tpu_custom_call" | custom-call | tf_op jit(solution)/shard_map/merge/pallas_call | solution.py:261
Async XLA Ops:
  0.0 48.3 %copy-start.2 = (bf16[2048,1,128]{2,0,1:T(8,128)(2,1)S(1)}, bf16[2048,1,128]{2,0,1:T(8,128)(2,1)}, u32[]{:S(2)}) copy-start(bf16[2048,1,128]{2,0,1:T(8,128)(2,1)} %param.9) | copy-start | bytes 1572868
  0.0 20.2 %collective-permute-start = (bf16[2048,128]{1,0:T(8,128)(2,1)}, bf16[2048,128]{1,0:T(8,128)(2,1)S(1)}, u32[]{:S(2)}, u32[]{:S(2)}) collective-permute-start(bf16[2048,128]{1,0:T(8,128)(2,1)} %bitcast.26), channel_id=1, source_target_pairs={{0,64},{64,128},{128,192},{192,0},{1,65},{65,129},{129,193},{193,1... | collective-permute-start | bytes 1572872 | tf_op jit(solution)/shard_map/ppermute | solution.py:278
  2.0 22.2 %collective-permute-start.1 = (bf16[2048,128]{1,0:T(8,128)(2,1)}, bf16[2048,128]{1,0:T(8,128)(2,1)S(1)}, u32[]{:S(2)}, u32[]{:S(2)}) collective-permute-start(bf16[2048,128]{1,0:T(8,128)(2,1)} %bitcast.29), channel_id=1, source_target_pairs={{0,64},{64,128},{128,192},{192,0},{1,65},{65,129},{129,193},{193,1... | collective-permute-start | bytes 1572872 | tf_op jit(solution)/shard_map/ppermute | solution.py:278
  3.3 21.0 %collective-permute-start.2 = (bf16[2048,128]{1,0:T(8,128)(2,1)}, bf16[2048,128]{1,0:T(8,128)(2,1)S(1)}, u32[]{:S(2)}, u32[]{:S(2)}) collective-permute-start(bf16[2048,128]{1,0:T(8,128)(2,1)} %bitcast.27), channel_id=1, source_target_pairs={{0,192},{64,0},{128,64},{192,128},{1,193},{65,1},{129,65},{193,129... | collective-permute-start | bytes 1572872 | tf_op jit(solution)/shard_map/ppermute | solution.py:278
  4.7 22.2 %collective-permute-start.3 = (bf16[2048,128]{1,0:T(8,128)(2,1)}, bf16[2048,128]{1,0:T(8,128)(2,1)S(1)}, u32[]{:S(2)}, u32[]{:S(2)}) collective-permute-start(bf16[2048,128]{1,0:T(8,128)(2,1)} %bitcast.30), channel_id=1, source_target_pairs={{0,192},{64,0},{128,64},{192,128},{1,193},{65,1},{129,65},{193,129... | collective-permute-start | bytes 1572872 | tf_op jit(solution)/shard_map/ppermute | solution.py:278
  6.6 31.3 %all-to-all-start = ((bf16[64,32,128]{2,1,0:T(8,128)(2,1)}), bf16[64,32,128]{2,1,0:T(8,128)(2,1)S(1)}, u32[]{:S(2)}, u32[]{:S(2)}) async-start(bf16[64,32,128]{2,1,0:T(8,128)(2,1)} %bitcast.36), calls=%async_computation | async-start | bytes 1048576 | tf_op jit(solution)/shard_map/all_to_all | solution.py:296
  26.9 21.4 %collective-permute-start.4 = (bf16[2048,128]{1,0:T(8,128)(2,1)S(1)}, bf16[2048,128]{1,0:T(8,128)(2,1)}, u32[]{:S(2)}, u32[]{:S(2)}) collective-permute-start(bf16[2048,128]{1,0:T(8,128)(2,1)S(1)} %collective-permute-done.refs_1_), channel_id=1, source_target_pairs={{0,64},{64,128},{128,192},{192,0},{1,65},{65,129},{129,193},{193,1... | collective-permute-start | bytes 1572872 | tf_op jit(solution)/shard_map/ppermute | solution.py:278
  27.6 20.7 %collective-permute-start.5 = (bf16[2048,128]{1,0:T(8,128)(2,1)S(1)}, bf16[2048,128]{1,0:T(8,128)(2,1)}, u32[]{:S(2)}, u32[]{:S(2)}) collective-permute-start(bf16[2048,128]{1,0:T(8,128)(2,1)S(1)} %collective-permute-done.3.refs_4_), channel_id=1, source_target_pairs={{0,192},{64,0},{128,64},{192,128},{1,193},{65,1},{129,65},{193,129... | collective-permute-start | bytes 1572872 | tf_op jit(solution)/shard_map/ppermute | solution.py:278
  37.9 31.9 %copy-start.4 = (bf16[2,2,8192]{2,1,0:T(2,128)(2,1)S(1)}, bf16[2,2,8192]{2,1,0:T(2,128)(2,1)}, u32[]{:S(2)}) copy-start(bf16[2,2,8192]{2,1,0:T(2,128)(2,1)} %param.8) | copy-start | bytes 196612
  37.9 31.9 %copy-start.5 = (bf16[2,2,8,128]{3,2,1,0:T(8,128)(2,1)S(1)}, bf16[2,2,8,128]{3,2,1,0:T(8,128)(2,1)}, u32[]{:S(2)}) copy-start(bf16[2,2,8,128]{3,2,1,0:T(8,128)(2,1)} %param.13) | copy-start | bytes 24580
  37.9 31.9 %copy-start.6 = (bf16[2,2,8,128]{3,2,1,0:T(8,128)(2,1)S(1)}, bf16[2,2,8,128]{3,2,1,0:T(8,128)(2,1)}, u32[]{:S(2)}) copy-start(bf16[2,2,8,128]{3,2,1,0:T(8,128)(2,1)} %param.14) | copy-start | bytes 24580
  37.9 31.9 %copy-start.7 = (s32[2]{0:T(128)S(1)}, s32[2]{0:T(128)}, u32[]{:S(2)}) copy-start(s32[2]{0:T(128)} %len_ref.1) | copy-start | bytes 28
  48.3 1.0 %copy-start.3 = (bf16[2048,1,128]{2,0,1:T(8,128)(2,1)S(1)}, bf16[2048,1,128]{2,0,1:T(8,128)(2,1)}, u32[]{:S(2)}) copy-start(bf16[2048,1,128]{2,0,1:T(8,128)(2,1)} %param.10) | copy-start | bytes 1572868
  63.6 26.4 %all-to-all-start.1 = ((bf16[64,40,128]{2,1,0:T(8,128)(2,1)}), bf16[64,40,128]{2,1,0:T(8,128)(2,1)S(1)}, u32[]{:S(2)}, u32[]{:S(2)}) async-start(bf16[64,40,128]{2,1,0:T(8,128)(2,1)} %prompt.3), calls=%async_computation.1 | async-start | bytes 1310720 | tf_op jit(solution)/shard_map/all_to_all | solution.py:314
  69.8 2.2 %copy-start = (bf16[2,1024,8,128]{3,2,1,0:T(8,128)(2,1)S(1)}, bf16[2,1024,8,128]{3,2,1,0:T(8,128)(2,1)}, u32[]{:S(2)}) copy-start(bf16[2,1024,8,128]{3,2,1,0:T(8,128)(2,1)} %param.11) | copy-start | bytes 12582916
  72.0 2.2 %copy-start.1 = (bf16[2,1024,8,128]{3,2,1,0:T(8,128)(2,1)S(1)}, bf16[2,1024,8,128]{3,2,1,0:T(8,128)(2,1)}, u32[]{:S(2)}) copy-start(bf16[2,1024,8,128]{3,2,1,0:T(8,128)(2,1)} %param.12) | copy-start | bytes 12582916

commit v5 on v4

--- a/solution.py
+++ b/solution.py
@@ -279,9 +279,6 @@
 
     keys_left, values_left = shift(keys, 1), shift(values, 1)
     keys_right, values_right = shift(keys, -1), shift(values, -1)
-    keys_left, values_left, keys_right, values_right = lax.optimization_barrier(
-        (keys_left, values_left, keys_right, values_right)
-    )
     keys_far, values_far = shift(keys_left, 1), shift(values_right, -1)
 
     per_dest = samples * steps * per_group
@@ -309,8 +306,10 @@
     def prompt(some_keys, some_values, late, carry, final, sub):
         return prompt_call(rows, some_keys, some_values, late, carry, final, sub, 2048, scale, per_dest)
 
-    carry = prompt([keys_left, keys_right], [values_left, values_right], (), None, False, 256)
-    coded = prompt([keys, keys_far], [values, values_far], (1, 3), carry, True, 128)
+    carry = prompt([keys], [values], (), None, False, 256)
+    coded = prompt(
+        [keys_left, keys_right, keys_far], [values_left, values_right, values_far], (2, 5), carry, True, 128
+    )
     got = lax.all_to_all(coded, ("z", "dec"), 0, 0, tiled=True)
     out = merge_call(got, own, own_level, z_size, groups)
     return (

time: 92.1 us -> 98.2 us (1.066)
  starting transfers between devices: 27.2 us -> 32.2 us
  local copies, waits for them, and re-layouts: 7.15 us -> 8.21 us
    all_to_all x1, starting transfers between devices: 6.09 us -> 11.6 us  [local(): got = lax.all_to_all(coded, ('z', 'dec'), 0, 0, tiled=True)]
    ppermute x6, waiting for transfers between devices: 6.72 us -> 1.51 us  [shift(): lax.ppermute(array, 'x', [(i, (i + amount) % x_size) for i in range(x_siz...]
    all_to_all x1, waiting for transfers between devices: 8.32 us -> 13.5 us  [local(): lax.all_to_all(spread, ('z', 'dec'), 0, 0, tiled=True).reshape(-1, head_dim)]
    unnamed x16, local copies, waits for them, and re-layouts: 5.43 us -> 6.48 us
  transfers between devices with their start and end apart: 8 -> 8, of which waited for: 4 -> 3; matrix products, arithmetic and copies ran while one was open for 2% -> 2% of each run, Pallas kernels for 17% -> 11%
where the time goes in v5:
time: 98.2 us; the launch traced here: 97.8 us
  starting transfers between devices  32.2 us (33%)
  Pallas kernels  31.7 us (32%)
  waiting for transfers between devices  25.5 us (26%)
  local copies, waits for them, and re-layouts  8.21 us (8%)
    pallas_call x2, Pallas kernels, prompt_call(): pl.pallas_call(functools.partial(prompt_kernel, blocks, late, scale, bool...  24.6 us
    all_to_all x1, waiting for transfers between devices, local(): lax.all_to_all(spread, ('z', 'dec'), 0, 0, tiled=True).reshape(-1, head_dim)  13.5 us
    all_to_all x1, starting transfers between devices, local(): lax.all_to_all(spread, ('z', 'dec'), 0, 0, tiled=True).reshape(-1, head_dim)  13.1 us
    all_to_all x1, starting transfers between devices, local(): got = lax.all_to_all(coded, ('z', 'dec'), 0, 0, tiled=True)  11.6 us
    all_to_all x1, waiting for transfers between devices, local(): got = lax.all_to_all(coded, ('z', 'dec'), 0, 0, tiled=True)  10.5 us
    ppermute x6, starting transfers between devices, shift(): lax.ppermute(array, 'x', [(i, (i + amount) % x_size) for i in range(x_siz...  7.53 us
    unnamed x16, local copies, waits for them, and re-layouts  6.48 us
    pallas_call x1, Pallas kernels, suffix_call(): pl.pallas_call(functools.partial(suffix_kernel, scale, groups, steps), gr...  5.4 us
  transfers between devices with their start and end apart: 8, of which 3 were waited for; matrix products, arithmetic and copies ran while one was open for 2% of the time, Pallas kernels for 11%

profile of v5, /device:TPU:1, one launch (start us, length us, event | category | flops | bytes accessed | tf_op | source)
XLA Modules:
  0.0 97.8 jit_solution(4144640088294195328)
XLA Ops:
  0.0 2.0 %collective-permute-start = (bf16[2048,128]{1,0:T(8,128)(2,1)}, bf16[2048,128]{1,0:T(8,128)(2,1)S(1)}, u32[]{:S(2)}, u32[]{:S(2)}) collective-permute-start(bf16[2048,128]{1,0:T(8,128)(2,1)} %bitcast.26), channel_id=1, source_target_pairs={{0,64},{64,128},{128,192},{192,0},{1,65},{65,129},{129,193},{193,1... | collective-permute-start | bytes 1572872 | tf_op jit(solution)/shard_map/ppermute | solution.py:278
  2.0 1.3 %collective-permute-start.4 = (bf16[2048,128]{1,0:T(8,128)(2,1)}, bf16[2048,128]{1,0:T(8,128)(2,1)S(1)}, u32[]{:S(2)}, u32[]{:S(2)}) collective-permute-start(bf16[2048,128]{1,0:T(8,128)(2,1)} %bitcast.29), channel_id=1, source_target_pairs={{0,192},{64,0},{128,64},{192,128},{1,193},{65,1},{129,65},{193,129... | collective-permute-start | bytes 1572872 | tf_op jit(solution)/shard_map/ppermute | solution.py:278
  3.3 0.8 copy.10
  4.2 0.9 broadcast_in_dim.2
  5.0 13.1 %all-to-all-start = ((bf16[64,32,128]{2,1,0:T(8,128)(2,1)}), bf16[64,32,128]{2,1,0:T(8,128)(2,1)S(1)}, u32[]{:S(2)}, u32[]{:S(2)}) async-start(bf16[64,32,128]{2,1,0:T(8,128)(2,1)} %bitcast.4), calls=%async_computation | async-start | bytes 1048576 | tf_op jit(solution)/shard_map/all_to_all | solution.py:293
  18.1 1.3 %collective-permute-start.1 = (bf16[2048,128]{1,0:T(8,128)(2,1)}, bf16[2048,128]{1,0:T(8,128)(2,1)S(1)}, u32[]{:S(2)}, u32[]{:S(2)}) collective-permute-start(bf16[2048,128]{1,0:T(8,128)(2,1)} %bitcast.27), channel_id=1, source_target_pairs={{0,192},{64,0},{128,64},{192,128},{1,193},{65,1},{129,65},{193,129... | collective-permute-start | bytes 1572872 | tf_op jit(solution)/shard_map/ppermute | solution.py:278
  19.5 0.2 collective-permute-start.3
  19.7 0.0 collective-permute-done.refs_1_
  19.7 0.0 collective-permute-start.2
  19.7 0.0 collective-permute-done.4.refs_5_
  19.7 2.6 %collective-permute-start.5 = (bf16[2048,128]{1,0:T(8,128)(2,1)S(1)}, bf16[2048,128]{1,0:T(8,128)(2,1)}, u32[]{:S(2)}, u32[]{:S(2)}) collective-permute-start(bf16[2048,128]{1,0:T(8,128)(2,1)S(1)} %collective-permute-done.4.refs_5_), channel_id=1, source_target_pairs={{0,192},{64,0},{128,64},{192,128},{1,193},{65,1},{129,65},{193,129... | collective-permute-start | bytes 1572872 | tf_op jit(solution)/shard_map/ppermute | solution.py:278
  22.4 13.5 %all-to-all-done = bf16[64,32,128]{2,1,0:T(8,128)(2,1)S(1)} async-done(((bf16[64,32,128]{2,1,0:T(8,128)(2,1)}), bf16[64,32,128]{2,1,0:T(8,128)(2,1)S(1)}, u32[]{:S(2)}, u32[]{:S(2)}) %all-to-all-start) | async-done | bytes 524320 | tf_op jit(solution)/shard_map/all_to_all | solution.py:293
  35.8 0.0 copy-start.2
  35.9 1.0 %copy-done.2 = bf16[2048,1,128]{2,0,1:T(8,128)(2,1)S(1)} copy-done((bf16[2048,1,128]{2,0,1:T(8,128)(2,1)S(1)}, bf16[2048,1,128]{2,0,1:T(8,128)(2,1)}, u32[]{:S(2)}) %copy-start.2) | copy-done | bytes 524312
  36.9 0.0 copy-start.3
  36.9 1.0 %copy-done.3 = bf16[2048,1,128]{2,0,1:T(8,128)(2,1)S(1)} copy-done((bf16[2048,1,128]{2,0,1:T(8,128)(2,1)S(1)}, bf16[2048,1,128]{2,0,1:T(8,128)(2,1)}, u32[]{:S(2)}) %copy-start.3) | copy-done | bytes 524312
  37.9 5.3 %prompt.2 = (f32[2048,128]{1,0:T(8,128)S(1)}, f32[2048,128]{1,0:T(8,128)S(1)}) custom-call(bf16[2048,128]{1,0:T(8,128)(2,1)S(1)} %bitcast.22, bf16[2048,128]{1,0:T(8,128)(2,1)S(1)} %bitcast.28, bf16[2048,128]{1,0:T(8,128)(2,1)S(1)} %bitcast.31), custom_call_target="tpu_custom_call" | custom-call | flops 4194304 | bytes 2621440 | tf_op jit(solution)/shard_map/prompt/pallas_call | solution.py:134
  43.3 0.0 copy-start.4
  43.3 0.0 copy-start.5
  43.3 0.0 copy-start.6
  43.3 0.0 copy-start.7
  43.3 0.0 collective-permute-done.1.refs_2_
  43.3 0.0 collective-permute-done.3.refs_4_
  43.4 1.5 %collective-permute-done.2.refs_3_ = bf16[2048,128]{1,0:T(8,128)(2,1)S(1)} collective-permute-done((bf16[2048,128]{1,0:T(8,128)(2,1)S(1)}, bf16[2048,128]{1,0:T(8,128)(2,1)S(1)}, u32[]{:S(2)}, u32[]{:S(2)}) %collective-permute-start.2) | collective-permute-done | bytes 524320 | tf_op jit(solution)/shard_map/ppermute | solution.py:278
  44.9 0.0 collective-permute-done.5.refs_6_
  44.9 19.3 %prompt.3 = bf16[64,40,128]{2,1,0:T(8,128)(2,1)} custom-call(bf16[2048,128]{1,0:T(8,128)(2,1)S(1)} %bitcast.23, bf16[2048,128]{1,0:T(8,128)(2,1)S(1)} %collective-permute-done.refs_1_, bf16[2048,128]{1,0:T(8,128)(2,1)S(1)} %collective-permute-done.1.refs_2_, bf16[2048,128]{1,0:T(8,128)(2,1)S(1)} %collective-permute-done.2.refs_3_, ...), custom_call_target="tpu_custom_call" | custom-call | flops 12582912 | bytes 4718592 | tf_op jit(solution)/shard_map/prompt/pallas_call | solution.py:134
  64.2 11.6 %all-to-all-start.1 = ((bf16[64,40,128]{2,1,0:T(8,128)(2,1)}), bf16[64,40,128]{2,1,0:T(8,128)(2,1)S(1)}, u32[]{:S(2)}, u32[]{:S(2)}) async-start(bf16[64,40,128]{2,1,0:T(8,128)(2,1)} %prompt.3), calls=%async_computation.1 | async-start | bytes 1310720 | tf_op jit(solution)/shard_map/all_to_all | solution.py:313
  75.7 0.0 copy-done.4
  75.8 0.0 copy-done.5
  75.8 0.0 copy-done.6
  75.8 0.0 copy-done.7
  75.8 0.0 copy-start
  75.8 2.2 %copy-done = bf16[2,1024,8,128]{3,2,1,0:T(8,128)(2,1)S(1)} copy-done((bf16[2,1024,8,128]{3,2,1,0:T(8,128)(2,1)S(1)}, bf16[2,1024,8,128]{3,2,1,0:T(8,128)(2,1)}, u32[]{:S(2)}) %copy-start) | copy-done | bytes 4194328
  78.0 0.0 copy-start.1
  78.0 2.2 %copy-done.1 = bf16[2,1024,8,128]{3,2,1,0:T(8,128)(2,1)S(1)} copy-done((bf16[2,1024,8,128]{3,2,1,0:T(8,128)(2,1)S(1)}, bf16[2,1024,8,128]{3,2,1,0:T(8,128)(2,1)}, u32[]{:S(2)}) %copy-start.1) | copy-done | bytes 4194328
  80.2 5.4 %suffix.1 = (f32[2,128,128]{2,1,0:T(8,128)S(1)}, f32[2,128,128]{2,1,0:T(8,128)S(1)}) custom-call(bf16[2,128,128]{2,1,0:T(8,128)(2,1)S(1)} %bitcast.33, bf16[2,8192,128]{2,1,0:T(8,128)(2,1)S(1)} %bitcast.24, bf16[2,8192,128]{2,1,0:T(8,128)(2,1)S(1)} %bitcast.25, bf16[2,16,128]{2,1,0:T(8,128)(2,1)S(1)} %bitcast.34, bf16[2,16,128]{2,1,0:T(8,128)(2,1)S(1)} %bitcast.35, ...), custom_call_target="tpu_custom_call" | custom-call | flops 1073741824 | bytes 8388608 | tf_op jit(solution)/shard_map/suffix/pallas_call | solution.py:201
  85.6 10.5 %all-to-all-done.1.got_ref = bf16[64,40,128]{2,1,0:T(8,128)(2,1)S(1)} async-done(((bf16[64,40,128]{2,1,0:T(8,128)(2,1)}), bf16[64,40,128]{2,1,0:T(8,128)(2,1)S(1)}, u32[]{:S(2)}, u32[]{:S(2)}) %all-to-all-start.1) | async-done | bytes 655392 | tf_op jit(solution)/shard_map/all_to_all | solution.py:313
  96.1 1.6 %merge.1 = bf16[2,128,128]{2,1,0:T(8,128)(2,1)} custom-call(bf16[64,40,128]{2,1,0:T(8,128)(2,1)S(1)} %all-to-all-done.1.got_ref, f32[2,128,128]{2,1,0:T(8,128)S(1)} %get-tuple-element.11.own_ref, f32[2,128,128]{2,1,0:T(8,128)S(1)} %get-tuple-element.12.own_level_ref), custom_call_target="tpu_custom_call" | custom-call | tf_op jit(solution)/shard_map/merge/pallas_call | solution.py:261
Async XLA Ops:
  0.0 19.7 %collective-permute-start = (bf16[2048,128]{1,0:T(8,128)(2,1)}, bf16[2048,128]{1,0:T(8,128)(2,1)S(1)}, u32[]{:S(2)}, u32[]{:S(2)}) collective-permute-start(bf16[2048,128]{1,0:T(8,128)(2,1)} %bitcast.26), channel_id=1, source_target_pairs={{0,64},{64,128},{128,192},{192,0},{1,65},{65,129},{129,193},{193,1... | collective-permute-start | bytes 1572872 | tf_op jit(solution)/shard_map/ppermute | solution.py:278
  2.0 17.7 %collective-permute-start.4 = (bf16[2048,128]{1,0:T(8,128)(2,1)}, bf16[2048,128]{1,0:T(8,128)(2,1)S(1)}, u32[]{:S(2)}, u32[]{:S(2)}) collective-permute-start(bf16[2048,128]{1,0:T(8,128)(2,1)} %bitcast.29), channel_id=1, source_target_pairs={{0,192},{64,0},{128,64},{192,128},{1,193},{65,1},{129,65},{193,129... | collective-permute-start | bytes 1572872 | tf_op jit(solution)/shard_map/ppermute | solution.py:278
  5.0 30.8 %all-to-all-start = ((bf16[64,32,128]{2,1,0:T(8,128)(2,1)}), bf16[64,32,128]{2,1,0:T(8,128)(2,1)S(1)}, u32[]{:S(2)}, u32[]{:S(2)}) async-start(bf16[64,32,128]{2,1,0:T(8,128)(2,1)} %bitcast.4), calls=%async_computation | async-start | bytes 1048576 | tf_op jit(solution)/shard_map/all_to_all | solution.py:293
  18.1 25.2 %collective-permute-start.1 = (bf16[2048,128]{1,0:T(8,128)(2,1)}, bf16[2048,128]{1,0:T(8,128)(2,1)S(1)}, u32[]{:S(2)}, u32[]{:S(2)}) collective-permute-start(bf16[2048,128]{1,0:T(8,128)(2,1)} %bitcast.27), channel_id=1, source_target_pairs={{0,192},{64,0},{128,64},{192,128},{1,193},{65,1},{129,65},{193,129... | collective-permute-start | bytes 1572872 | tf_op jit(solution)/shard_map/ppermute | solution.py:278
  19.5 23.9 %collective-permute-start.3 = (bf16[2048,128]{1,0:T(8,128)(2,1)}, bf16[2048,128]{1,0:T(8,128)(2,1)S(1)}, u32[]{:S(2)}, u32[]{:S(2)}) collective-permute-start(bf16[2048,128]{1,0:T(8,128)(2,1)} %bitcast.30), channel_id=1, source_target_pairs={{0,64},{64,128},{128,192},{192,0},{1,65},{65,129},{129,193},{193,1... | collective-permute-start | bytes 1572872 | tf_op jit(solution)/shard_map/ppermute | solution.py:278
  19.7 25.2 %collective-permute-start.2 = (bf16[2048,128]{1,0:T(8,128)(2,1)S(1)}, bf16[2048,128]{1,0:T(8,128)(2,1)S(1)}, u32[]{:S(2)}, u32[]{:S(2)}) collective-permute-start(bf16[2048,128]{1,0:T(8,128)(2,1)S(1)} %collective-permute-done.refs_1_), channel_id=1, source_target_pairs={{0,64},{64,128},{128,192},{192,0},{1,65},{65,129},{129,193},{193,1... | collective-permute-start | bytes 1572872 | tf_op jit(solution)/shard_map/ppermute | solution.py:278
  19.7 25.1 %collective-permute-start.5 = (bf16[2048,128]{1,0:T(8,128)(2,1)S(1)}, bf16[2048,128]{1,0:T(8,128)(2,1)}, u32[]{:S(2)}, u32[]{:S(2)}) collective-permute-start(bf16[2048,128]{1,0:T(8,128)(2,1)S(1)} %collective-permute-done.4.refs_5_), channel_id=1, source_target_pairs={{0,192},{64,0},{128,64},{192,128},{1,193},{65,1},{129,65},{193,129... | collective-permute-start | bytes 1572872 | tf_op jit(solution)/shard_map/ppermute | solution.py:278
  35.8 1.0 %copy-start.2 = (bf16[2048,1,128]{2,0,1:T(8,128)(2,1)S(1)}, bf16[2048,1,128]{2,0,1:T(8,128)(2,1)}, u32[]{:S(2)}) copy-start(bf16[2048,1,128]{2,0,1:T(8,128)(2,1)} %param.9) | copy-start | bytes 1572868
  36.9 1.0 %copy-start.3 = (bf16[2048,1,128]{2,0,1:T(8,128)(2,1)S(1)}, bf16[2048,1,128]{2,0,1:T(8,128)(2,1)}, u32[]{:S(2)}) copy-start(bf16[2048,1,128]{2,0,1:T(8,128)(2,1)} %param.10) | copy-start | bytes 1572868
  43.3 32.5 %copy-start.4 = (bf16[2,2,8192]{2,1,0:T(2,128)(2,1)S(1)}, bf16[2,2,8192]{2,1,0:T(2,128)(2,1)}, u32[]{:S(2)}) copy-start(bf16[2,2,8192]{2,1,0:T(2,128)(2,1)} %param.8) | copy-start | bytes 196612
  43.3 32.5 %copy-start.5 = (bf16[2,2,8,128]{3,2,1,0:T(8,128)(2,1)S(1)}, bf16[2,2,8,128]{3,2,1,0:T(8,128)(2,1)}, u32[]{:S(2)}) copy-start(bf16[2,2,8,128]{3,2,1,0:T(8,128)(2,1)} %param.13) | copy-start | bytes 24580
  43.3 32.5 %copy-start.6 = (bf16[2,2,8,128]{3,2,1,0:T(8,128)(2,1)S(1)}, bf16[2,2,8,128]{3,2,1,0:T(8,128)(2,1)}, u32[]{:S(2)}) copy-start(bf16[2,2,8,128]{3,2,1,0:T(8,128)(2,1)} %param.14) | copy-start | bytes 24580
  43.3 32.4 %copy-start.7 = (s32[2]{0:T(128)S(1)}, s32[2]{0:T(128)}, u32[]{:S(2)}) copy-start(s32[2]{0:T(128)} %len_ref.1) | copy-start | bytes 28
  64.2 31.9 %all-to-all-start.1 = ((bf16[64,40,128]{2,1,0:T(8,128)(2,1)}), bf16[64,40,128]{2,1,0:T(8,128)(2,1)S(1)}, u32[]{:S(2)}, u32[]{:S(2)}) async-start(bf16[64,40,128]{2,1,0:T(8,128)(2,1)} %prompt.3), calls=%async_computation.1 | async-start | bytes 1310720 | tf_op jit(solution)/shard_map/all_to_all | solution.py:313
  75.8 2.2 %copy-start = (bf16[2,1024,8,128]{3,2,1,0:T(8,128)(2,1)S(1)}, bf16[2,1024,8,128]{3,2,1,0:T(8,128)(2,1)}, u32[]{:S(2)}) copy-start(bf16[2,1024,8,128]{3,2,1,0:T(8,128)(2,1)} %param.11) | copy-start | bytes 12582916
  78.0 2.2 %copy-start.1 = (bf16[2,1024,8,128]{3,2,1,0:T(8,128)(2,1)S(1)}, bf16[2,1024,8,128]{3,2,1,0:T(8,128)(2,1)}, u32[]{:S(2)}) copy-start(bf16[2,1024,8,128]{3,2,1,0:T(8,128)(2,1)} %param.12) | copy-start | bytes 12582916
